TPU v7x, 32 devices: a whole 2x2x4 slice. The times are simulated.
32 devices in a mesh: groups: 2 (over y), lon: 4 (over z), lat: 2 (over x), lev: 2 (over core).
Axes of the slice: x: 2, y: 2, z: 4, core: 2. Of those that a mesh axis runs over, the one named last changes fastest.
Arguments:
- state: float32 [4, 60, 64, 512], P('groups', 'lev', 'lat', 'lon'), parts along dimension 0, may hold values from -6 to 6
- winds: float32 [4, 60, 64, 512], P('groups', 'lev', 'lat', 'lon'), parts along dimension 0, may hold values from -0.25 to 0.25
- land_mask: int32 [128, 512], P(('groups', 'lat'), 'lon'), parts along dimension 0, may hold values 0 or 1
- first_weight: bfloat16 [1080, 512], replicated, may hold values from -0.1875 to 0.1875
- second_weight: bfloat16 [512, 512], replicated, may hold values from -0.25 to 0.25
- head_weight: bfloat16 [2, 512, 120], replicated, may hold values from -0.25 to 0.25
Outputs:
- state_next: float32 [4, 60, 64, 512], P('groups', 'lev', 'lat', 'lon'), parts along dimension 0
There are 2 independent parts, one for each index of `groups`. A program takes and returns all parts, laid end to end along the dimension named above; an argument that names none is the same for every part. Nothing has to cross between parts.
All inputs are finite; a program needn't handle non-finite values. No bound on the sum of `land_mask` on one device may be relied on, other than what follows from the above.
Results may differ from a plain program's by a relative error of at most 0.0016.
Values may be sent and summed in bfloat16 or wider, within the bound.
A program may use at most 64 MiB of HBM per device.

v0:
```python
import jax
import jax.numpy as jnp
from jax import lax
from jax.sharding import PartitionSpec as P

STEPS = 4


def with_halo(cells, sides, width, closed):
    for axis, dim in sides:
        count = lax.axis_size(axis)
        ends = count if closed else count - 1
        head = lax.slice_in_dim(cells, 0, width, axis=dim)
        tail = lax.slice_in_dim(cells, cells.shape[dim] - width, cells.shape[dim], axis=dim)
        cells = jnp.concatenate(
            [
                lax.ppermute(tail, axis, [(i, (i + 1) % count) for i in range(ends)]),
                cells,
                lax.ppermute(head, axis, [((i + 1) % count, i) for i in range(ends)]),
            ],
            axis=dim,
        )
    return cells


def pad_fields(field, width):
    beside_all = with_halo(field, (("lon", 3),), width, True)
    return with_halo(beside_all, (("lat", 2),), width, False)


def pad_columns(field):
    beside_all = with_halo(field, (("lon", 3),), 1, True)
    return with_halo(beside_all, (("lat", 2),), 1, False)


def substep(tracer, zonal, meridional):
    east = zonal[..., 1:-1, 1:]
    flux_x = (
        jnp.maximum(east, 0.0) * tracer[..., 1:-1, :-1]
        + jnp.minimum(east, 0.0) * tracer[..., 1:-1, 1:]
    )
    north = meridional[..., 1:, 1:-1]
    flux_y = (
        jnp.maximum(north, 0.0) * tracer[..., :-1, 1:-1]
        + jnp.minimum(north, 0.0) * tracer[..., 1:, 1:-1]
    )
    return (
        tracer[..., 1:-1, 1:-1]
        - (flux_x[..., 1:] - flux_x[..., :-1])
        - (flux_y[..., 1:, :] - flux_y[..., :-1, :])
    )


def neighbourhood(padded, row_count, col_count):
    parts = [padded[:, :, a : a + row_count, b : b + col_count] for a in range(3) for b in range(3)]
    return jnp.stack(parts, 0).reshape(-1, row_count * col_count)


def shards(state, winds, land_mask, first_weight, second_weight, head_weight):
    fields, levels_here, row_count, col_count = state.shape
    padded_winds = pad_fields(winds, 1)
    zonal = padded_winds[0:1]
    meridional = padded_winds[1:2]
    tracer = state
    for repeat in range(STEPS):
        tracer = substep(pad_fields(tracer, 1), zonal, meridional)
    padded_cols = pad_columns(tracer.astype(jnp.bfloat16))
    level_devices = lax.axis_size("lev")
    share = row_count // level_devices
    lev_index = lax.axis_index("lev")
    width = second_weight.shape[0]
    features = neighbourhood(padded_cols, row_count, col_count)
    local_weight = lax.dynamic_slice_in_dim(
        first_weight.reshape(9, fields, levels_here * level_devices, width),
        lev_index * levels_here,
        levels_here,
        2,
    ).reshape(-1, width)
    before = lax.psum_scatter(
        lax.dot_general(
            features, local_weight, (((0,), (0,)), ((), ())), preferred_element_type=jnp.float32
        ),
        "lev",
        scatter_dimension=0,
        tiled=True,
    )
    first = jax.nn.silu(before).astype(jnp.bfloat16)
    second = jax.nn.silu(jnp.dot(first, second_weight, preferred_element_type=jnp.float32)).astype(
        jnp.bfloat16
    )
    ocean = lax.dot_general(
        head_weight[0], second, (((0,), (1,)), ((), ())), preferred_element_type=jnp.float32
    )
    land = lax.dot_general(
        head_weight[1], second, (((0,), (1,)), ((), ())), preferred_element_type=jnp.float32
    )
    mask_rows = lax.dynamic_slice_in_dim(land_mask, lev_index * share, share, 0).reshape(1, -1)
    tendency = jnp.where(mask_rows == 1, land, ocean).reshape(
        fields, levels_here * level_devices, share, col_count
    )
    returned = lax.all_to_all(tendency, "lev", split_axis=1, concat_axis=2, tiled=True)
    return tracer + returned


def solution(mesh):
    placed = (
        P("groups", "lev", "lat", "lon"),
        P("groups", "lev", "lat", "lon"),
        P(("groups", "lat"), "lon"),
        P(),
        P(),
        P(),
    )
    return jax.shard_map(
        shards,
        mesh=mesh,
        in_specs=placed,
        out_specs=P("groups", "lev", "lat", "lon"),
        check_vma=False,
    )
```

profile of v0, /device:TPU:0, one launch (start us, length us, event | category | flops | bytes accessed | tf_op | source)
XLA Modules:
  0.0 200.3 jit_solution(6011274871800137987)
XLA Ops:
  6.5 1.9 fusion.49
  8.9 5.1 %collective-permute-start.2 = (f32[2,30,32,1]{2,1,3,0:T(8,128)S(1)}, f32[2,30,32,1]{2,1,3,0:T(8,128)S(1)}, u32[]{:S(2)}, u32[]{:S(2)}) collective-permute-start(f32[2,30,32,1]{2,1,3,0:T(8,128)S(1)} %copy.92), channel_id=1, source_target_pairs={{4,0},{8,4},{12,8},{0,12},{5,1},{9,5},{13,9},{1,13},{6,2},{10,6},{... | collective-permute-start | bytes 23048 | tf_op jit(solution)/shard_map/ppermute | solution.py:19
  16.3 2.3 %copy.90 = f32[2,30,32,1]{2,1,3,0:T(8,128)} copy(f32[2,30,32,1]{3,2,1,0:T(8,128)} %get-tuple-element.30) | data formatting | bytes 15360
  18.7 3.8 %collective-permute-start = (f32[2,30,32,1]{2,1,3,0:T(8,128)}, f32[2,30,32,1]{2,1,3,0:T(8,128)}, u32[]{:S(2)}, u32[]{:S(2)}) collective-permute-start(f32[2,30,32,1]{2,1,3,0:T(8,128)} %copy.90), channel_id=1, source_target_pairs={{4,0},{8,4},{12,8},{0,12},{5,1},{9,5},{13,9},{1,13},{6,2},{10,6},{... | collective-permute-start | bytes 23048 | tf_op jit(solution)/shard_map/ppermute | solution.py:19
  24.0 2.2 %copy.60 = f32[2,30,32,1]{3,2,1,0:T(8,128)} copy(f32[2,30,32,1]{2,1,3,0:T(8,128)} %collective-permute-done.1) | data formatting | bytes 15360 | tf_op jit(solution)/shard_map/ppermute | solution.py:17
  26.2 2.1 %pad_maximum_fusion.45 = (f32[2,30,1,130]{3,2,1,0:T(1,128)S(1)}, f32[2,30,1,130]{3,2,1,0:T(1,128)}) fusion(f32[2,30,32,1]{3,2,1,0:T(8,128)S(1)} %copy.62, f32[2,30,32,128]{3,2,1,0:T(8,128)S(1)} %copy-done.1, f32[2,30,32,1]{3,2,1,0:T(8,128)} %copy.60), kind=kLoop, calls=%fused_computation.118 | loop fusion | flops 31200 | bytes 1060800 | tf_op jit(solution)/shard_map/slice | solution.py:14
  29.6 5.8 %collective-permute-start.5 = (f32[2,30,1,130]{3,2,1,0:T(1,128)S(1)}, f32[2,30,1,130]{3,2,1,0:T(1,128)}, u32[]{:S(2)}, u32[]{:S(2)}) collective-permute-start(f32[2,30,1,130]{3,2,1,0:T(1,128)S(1)} %get-tuple-element.15), channel_id=1, source_target_pairs={{0,2},{1,3},{4,6},{5,7},{8,10},{9,11},{12,14},{13,15},{16,18},{17,... | collective-permute-start | bytes 93608 | tf_op jit(solution)/shard_map/ppermute | solution.py:17
  35.4 2.2 %copy.58 = f32[2,30,32,1]{3,2,1,0:T(8,128)} copy(f32[2,30,32,1]{2,1,3,0:T(8,128)} %collective-permute-done) | data formatting | bytes 15360 | tf_op jit(solution)/shard_map/ppermute | solution.py:19
  37.5 2.3 %maximum_bitcast_fusion = (f32[30,32,129]{2,1,0:T(8,128)S(1)}, f32[30,32,129]{2,1,0:T(8,128)}) fusion(f32[2,30,32,1]{3,2,1,0:T(8,128)} %copy.58, f32[2,30,32,128]{3,2,1,0:T(8,128)S(1)} %copy-done.2), kind=kLoop, calls=%fused_computation.74 | loop fusion | flops 371520 | bytes 1981440 | tf_op jit(solution)/shard_map/mul | solution.py:39
  39.8 2.1 %copy.64 = f32[2,30,32,1]{3,2,1,0:T(8,128)} copy(f32[2,30,32,1]{2,1,3,0:T(8,128)} %collective-permute-done.3) | data formatting | bytes 15360 | tf_op jit(solution)/shard_map/ppermute | solution.py:17
  41.9 1.5 pad_maximum_fusion.46
  43.4 1.3 collective-permute-start.4
  45.5 4.1 %collective-permute-done.4 = f32[2,30,1,130]{3,2,1,0:T(1,128)S(1)} collective-permute-done((f32[2,30,1,130]{3,2,1,0:T(1,128)S(1)}, f32[2,30,1,130]{3,2,1,0:T(1,128)S(1)}, u32[]{:S(2)}, u32[]{:S(2)}) %collective-permute-start.4) | collective-permute-done | bytes 31232 | tf_op jit(solution)/shard_map/ppermute | solution.py:19
  49.9 1.8 fusion.16
  53.5 1.6 copy.70
  55.1 3.9 %collective-permute-start.8 = (f32[2,30,32,1]{2,1,3,0:T(8,128)S(1)}, f32[2,30,32,1]{2,1,3,0:T(8,128)S(1)}, u32[]{:S(2)}, u32[]{:S(2)}) collective-permute-start(f32[2,30,32,1]{2,1,3,0:T(8,128)S(1)} %copy.70), channel_id=1, source_target_pairs={{4,0},{8,4},{12,8},{0,12},{5,1},{9,5},{13,9},{1,13},{6,2},{10,6},{... | collective-permute-start | bytes 23048 | tf_op jit(solution)/shard_map/ppermute | solution.py:19
  60.5 1.4 copy.71
  61.9 4.1 %collective-permute-done.7 = f32[2,30,32,1]{2,1,3,0:T(8,128)} collective-permute-done((f32[2,30,32,1]{2,1,3,0:T(8,128)}, f32[2,30,32,1]{2,1,3,0:T(8,128)}, u32[]{:S(2)}, u32[]{:S(2)}) %collective-permute-start.7) | collective-permute-done | bytes 7712 | tf_op jit(solution)/shard_map/ppermute | solution.py:17
  66.0 2.1 %copy.69 = f32[2,30,32,1]{3,2,1,0:T(8,128)} copy(f32[2,30,32,1]{2,1,3,0:T(8,128)} %collective-permute-done.7) | data formatting | bytes 15360 | tf_op jit(solution)/shard_map/ppermute | solution.py:17
  68.2 1.9 pad_maximum_fusion.42
  71.4 4.7 %collective-permute-start.9 = (f32[2,30,1,130]{3,2,1,0:T(1,128)S(1)}, f32[2,30,1,130]{3,2,1,0:T(1,128)S(1)}, u32[]{:S(2)}, u32[]{:S(2)}) collective-permute-start(f32[2,30,1,130]{3,2,1,0:T(1,128)S(1)} %get-tuple-element.13), channel_id=1, source_target_pairs={{0,2},{1,3},{4,6},{5,7},{8,10},{9,11},{12,14},{13,15},{16,18},{17,... | collective-permute-start | bytes 93608 | tf_op jit(solution)/shard_map/ppermute | solution.py:17
  80.5 1.6 copy.76
  83.3 1.9 collective-permute-start.11
  86.1 1.4 copy.77
  87.5 1.9 collective-permute-done.11
  89.4 2.1 %copy.75 = f32[2,30,32,1]{3,2,1,0:T(8,128)} copy(f32[2,30,32,1]{2,1,3,0:T(8,128)} %collective-permute-done.11) | data formatting | bytes 15360 | tf_op jit(solution)/shard_map/ppermute | solution.py:17
  91.5 1.9 pad_maximum_fusion.39
  94.7 4.9 %collective-permute-start.13 = (f32[2,30,1,130]{3,2,1,0:T(1,128)S(1)}, f32[2,30,1,130]{3,2,1,0:T(1,128)S(1)}, u32[]{:S(2)}, u32[]{:S(2)}) collective-permute-start(f32[2,30,1,130]{3,2,1,0:T(1,128)S(1)} %get-tuple-element.11), channel_id=1, source_target_pairs={{0,2},{1,3},{4,6},{5,7},{8,10},{9,11},{12,14},{13,15},{16,18},{17,... | collective-permute-start | bytes 93608 | tf_op jit(solution)/shard_map/ppermute | solution.py:17
  103.8 1.6 copy.82
  106.7 1.9 collective-permute-start.15
  109.4 1.4 copy.83
  110.8 1.9 collective-permute-done.15
  112.7 2.1 %copy.81 = f32[2,30,32,1]{3,2,1,0:T(8,128)} copy(f32[2,30,32,1]{2,1,3,0:T(8,128)} %collective-permute-done.15) | data formatting | bytes 15360 | tf_op jit(solution)/shard_map/ppermute | solution.py:17
  114.8 1.9 pad_maximum_fusion.36
  116.7 1.3 collective-permute-start.18
  118.1 4.7 %collective-permute-start.17 = (f32[2,30,1,130]{3,2,1,0:T(1,128)S(1)}, f32[2,30,1,130]{3,2,1,0:T(1,128)S(1)}, u32[]{:S(2)}, u32[]{:S(2)}) collective-permute-start(f32[2,30,1,130]{3,2,1,0:T(1,128)S(1)} %get-tuple-element.9), channel_id=1, source_target_pairs={{0,2},{1,3},{4,6},{5,7},{8,10},{9,11},{12,14},{13,15},{16,18},{17,... | collective-permute-start | bytes 93608 | tf_op jit(solution)/shard_map/ppermute | solution.py:17
  126.9 1.9 collective-permute-start.19
  128.9 2.2 %reshape.23 = bf16[9,2,60,512]{3,2,1,0:T(8,128)(2,1)} reshape(bf16[1080,512]{1,0:T(8,128)(2,1)} %param.9) | data formatting | bytes 2211840 | tf_op jit(solution)/shard_map/reshape | solution.py:74
  131.1 10.0 %collective-permute-done.20 = bf16[2,30,32,1]{3,2,1,0:T(8,128)(2,1)S(1)} collective-permute-done((bf16[2,30,32,1]{3,2,1,0:T(8,128)(2,1)}, bf16[2,30,32,1]{3,2,1,0:T(8,128)(2,1)S(1)}, u32[]{:S(2)}, u32[]{:S(2)}) %collective-permute-start.20) | collective-permute-done | bytes 3872 | tf_op jit(solution)/shard_map/ppermute | solution.py:19
  141.5 1.3 collective-permute-start.22
  142.8 4.8 %collective-permute-start.21 = (bf16[2,30,1,130]{3,2,1,0:T(2,128)(2,1)S(1)}, bf16[2,30,1,130]{3,2,1,0:T(2,128)(2,1)S(1)}, u32[]{:S(2)}, u32[]{:S(2)}) collective-permute-start(bf16[2,30,1,130]{3,2,1,0:T(2,128)(2,1)S(1)} %get-tuple-element.22), channel_id=1, source_target_pairs={{0,2},{1,3},{4,6},{5,7},{8,10},{9,11},{12,14},{13,15},{16,18},{17,... | collective-permute-start | bytes 46808 | tf_op jit(solution)/shard_map/ppermute | solution.py:17
  148.6 2.0 %reshape.24 = bf16[540,512]{1,0:T(8,128)(2,1)} reshape(bf16[9,2,30,512]{3,2,1,0:T(8,128)(2,1)} %constant_dynamic-slice_fusion) | data formatting | bytes 1105920 | tf_op jit(solution)/shard_map/reshape | solution.py:78
  150.7 1.5 pad_maximum_fusion.24
  155.8 4.4 %copy.94 = bf16[68,8,32,128]{3,1,2,0:T(8,128)(2,1)S(1)} copy(bf16[68,8,32,128]{3,2,1,0:T(8,128)(2,1)S(1)} %bitcast.69) | data formatting | bytes 8912896
  160.2 6.0 %fusion.51 = f32[4096,512]{1,0:T(8,128)} fusion(bf16[540,4096]{1,0:T(8,128)(2,1)S(1)} %bitcast.71, bf16[540,512]{1,0:T(8,128)(2,1)S(1)} %copy-done.27), kind=kOutput, calls=%fused_computation.132 | convolution fusion | flops 2264924160 | bytes 13365248 | tf_op jit(solution)/shard_map/dot_general | solution.py:80
  167.0 14.3 %reduce-scatter.2.cloned.1.call-done = f32[2048,512]{1,0:T(8,128)} async-done(((f32[4096,512]{1,0:T(8,128)}), f32[2048,512]{1,0:T(8,128)}) %reduce-scatter.2.cloned.1.call-update) | async-done | bytes 4194320 | tf_op jit(solution)/shard_map/reduce_scatter | solution.py:79
  181.3 4.4 %multiply_convert_fusion = bf16[2048,512]{1,0:T(8,128)(2,1)S(1)} fusion(bf16[512,512]{1,0:T(8,128)(2,1)S(1)} %copy-done, f32[2048,512]{1,0:T(8,128)} %reduce-scatter.2.cloned.1.call-done), kind=kOutput, calls=%fused_computation | convolution fusion | flops 1084227584 | bytes 6815744 | tf_op jit(solution)/shard_map/dot_general | solution.py:88
  187.7 4.5 %all_to_all.18 = f32[2,60,16,128]{3,2,0,1:T(8,128)S(1)} all-to-all(f32[2,60,16,128]{3,2,0,1:T(8,128)S(1)} %copy.86), channel_id=1, replica_groups=mesh['groups'=2,'lon'=4,'lat'=2,'lev'=2] {'lev'}, dimensions={1} | all-to-all | bytes 1966080 | tf_op jit(solution)/shard_map/all_to_all | solution.py:101
  (133 shorter events, 38.1 us)
Async XLA Ops:
  6.5 174.8 %copy-start = (bf16[512,512]{1,0:T(8,128)(2,1)S(1)}, bf16[512,512]{1,0:T(8,128)(2,1)}, u32[]{:S(2)}) copy-start(bf16[512,512]{1,0:T(8,128)(2,1)} %param.10) | copy-start | bytes 1572868
  6.5 174.8 %reduce-scatter.2.cloned.1.call-start = ((), (), s32[]{:S(2)}) async-start(), calls=%async_computation.2 | async-start | bytes 12582912 | tf_op jit(solution)/shard_map/reduce_scatter | solution.py:79
  8.5 6.6 %copy-start.2 = (f32[2,30,32,128]{3,2,1,0:T(8,128)S(1)}, f32[2,30,32,128]{3,2,1,0:T(8,128)}, u32[]{:S(2)}) copy-start(f32[2,30,32,128]{3,2,1,0:T(8,128)} %param.7) | copy-start | bytes 2949124
  8.9 14.6 %collective-permute-start.2 = (f32[2,30,32,1]{2,1,3,0:T(8,128)S(1)}, f32[2,30,32,1]{2,1,3,0:T(8,128)S(1)}, u32[]{:S(2)}, u32[]{:S(2)}) collective-permute-start(f32[2,30,32,1]{2,1,3,0:T(8,128)S(1)} %copy.92), channel_id=1, source_target_pairs={{4,0},{8,4},{12,8},{0,12},{5,1},{9,5},{13,9},{1,13},{6,2},{10,6},{... | collective-permute-start | bytes 23048 | tf_op jit(solution)/shard_map/ppermute | solution.py:19
  15.0 8.9 %collective-permute-start.1 = (f32[2,30,32,1]{2,1,3,0:T(8,128)}, f32[2,30,32,1]{2,1,3,0:T(8,128)}, u32[]{:S(2)}, u32[]{:S(2)}) collective-permute-start(f32[2,30,32,1]{2,1,3,0:T(8,128)} %copy.91), channel_id=1, source_target_pairs={{0,4},{4,8},{8,12},{12,0},{1,5},{5,9},{9,13},{13,1},{2,6},{6,10},{... | collective-permute-start | bytes 23048 | tf_op jit(solution)/shard_map/ppermute | solution.py:17
  16.3 9.8 %copy-start.1 = (f32[2,30,32,128]{3,2,1,0:T(8,128)S(1)}, f32[2,30,32,128]{3,2,1,0:T(8,128)}, u32[]{:S(2)}) copy-start(f32[2,30,32,128]{3,2,1,0:T(8,128)} %param.6) | copy-start | bytes 2949124
  18.7 16.7 %collective-permute-start = (f32[2,30,32,1]{2,1,3,0:T(8,128)}, f32[2,30,32,1]{2,1,3,0:T(8,128)}, u32[]{:S(2)}, u32[]{:S(2)}) collective-permute-start(f32[2,30,32,1]{2,1,3,0:T(8,128)} %copy.90), channel_id=1, source_target_pairs={{4,0},{8,4},{12,8},{0,12},{5,1},{9,5},{13,9},{1,13},{6,2},{10,6},{... | collective-permute-start | bytes 23048 | tf_op jit(solution)/shard_map/ppermute | solution.py:19
  23.5 16.3 %collective-permute-start.3 = (f32[2,30,32,1]{2,1,3,0:T(8,128)}, f32[2,30,32,1]{2,1,3,0:T(8,128)}, u32[]{:S(2)}, u32[]{:S(2)}) collective-permute-start(f32[2,30,32,1]{2,1,3,0:T(8,128)} %copy.93), channel_id=1, source_target_pairs={{0,4},{4,8},{8,12},{12,0},{1,5},{5,9},{9,13},{13,1},{2,6},{6,10},{... | collective-permute-start | bytes 23048 | tf_op jit(solution)/shard_map/ppermute | solution.py:17
  24.0 4.3 %copy-start.7 = (f32[2,30,32,1]{3,2,1,0:T(8,128)}, f32[2,30,32,1]{3,2,1,0:T(8,128)S(1)}, u32[]{:S(2)}) copy-start(f32[2,30,32,1]{3,2,1,0:T(8,128)S(1)} %copy.62) | copy-start | bytes 23044
  28.3 21.6 %collective-permute-start.6 = (f32[2,30,1,130]{3,2,1,0:T(1,128)}, f32[2,30,1,130]{3,2,1,0:T(1,128)}, u32[]{:S(2)}, u32[]{:S(2)}) collective-permute-start(f32[2,30,1,130]{3,2,1,0:T(1,128)} %get-tuple-element.16), channel_id=1, source_target_pairs={{2,0},{3,1},{6,4},{7,5},{10,8},{11,9},{14,12},{15,13},{18,16},{19,... | collective-permute-start | bytes 93608 | tf_op jit(solution)/shard_map/ppermute | solution.py:19
  29.6 20.3 %collective-permute-start.5 = (f32[2,30,1,130]{3,2,1,0:T(1,128)S(1)}, f32[2,30,1,130]{3,2,1,0:T(1,128)}, u32[]{:S(2)}, u32[]{:S(2)}) collective-permute-start(f32[2,30,1,130]{3,2,1,0:T(1,128)S(1)} %get-tuple-element.15), channel_id=1, source_target_pairs={{0,2},{1,3},{4,6},{5,7},{8,10},{9,11},{12,14},{13,15},{16,18},{17,... | collective-permute-start | bytes 93608 | tf_op jit(solution)/shard_map/ppermute | solution.py:17
  43.4 6.1 %collective-permute-start.4 = (f32[2,30,1,130]{3,2,1,0:T(1,128)S(1)}, f32[2,30,1,130]{3,2,1,0:T(1,128)S(1)}, u32[]{:S(2)}, u32[]{:S(2)}) collective-permute-start(f32[2,30,1,130]{3,2,1,0:T(1,128)S(1)} %pad_maximum_fusion.46), channel_id=1, source_target_pairs={{2,0},{3,1},{6,4},{7,5},{10,8},{11,9},{14,12},{15,13},{18,16},{19,... | collective-permute-start | bytes 93608 | tf_op jit(solution)/shard_map/ppermute | solution.py:19
  44.7 4.8 %copy-start.16 = (f32[2,30,32,1]{3,2,1,0:T(8,128)S(1)}, f32[2,30,32,1]{3,2,1,0:T(8,128)}, u32[]{:S(2)}) copy-start(f32[2,30,32,1]{3,2,1,0:T(8,128)} %copy.58) | copy-start | bytes 23044
  44.8 4.8 %copy-start.25 = (f32[2,30,32,1]{3,2,1,0:T(8,128)S(1)}, f32[2,30,32,1]{3,2,1,0:T(8,128)}, u32[]{:S(2)}) copy-start(f32[2,30,32,1]{3,2,1,0:T(8,128)} %copy.64) | copy-start | bytes 23044
  55.1 5.5 %collective-permute-start.8 = (f32[2,30,32,1]{2,1,3,0:T(8,128)S(1)}, f32[2,30,32,1]{2,1,3,0:T(8,128)S(1)}, u32[]{:S(2)}, u32[]{:S(2)}) collective-permute-start(f32[2,30,32,1]{2,1,3,0:T(8,128)S(1)} %copy.70), channel_id=1, source_target_pairs={{4,0},{8,4},{12,8},{0,12},{5,1},{9,5},{13,9},{1,13},{6,2},{10,6},{... | collective-permute-start | bytes 23048 | tf_op jit(solution)/shard_map/ppermute | solution.py:19
  60.0 6.0 %collective-permute-start.7 = (f32[2,30,32,1]{2,1,3,0:T(8,128)}, f32[2,30,32,1]{2,1,3,0:T(8,128)}, u32[]{:S(2)}, u32[]{:S(2)}) collective-permute-start(f32[2,30,32,1]{2,1,3,0:T(8,128)} %copy.68), channel_id=1, source_target_pairs={{0,4},{4,8},{8,12},{12,0},{1,5},{5,9},{9,13},{13,1},{2,6},{6,10},{... | collective-permute-start | bytes 23048 | tf_op jit(solution)/shard_map/ppermute | solution.py:17
  61.9 14.2 %copy-start.4 = (f32[30,32,129]{2,1,0:T(8,128)S(1)}, f32[30,32,129]{2,1,0:T(8,128)}, u32[]{:S(2)}) copy-start(f32[30,32,129]{2,1,0:T(8,128)} %get-tuple-element.18) | copy-start | bytes 1486084
  68.2 7.9 %copy-start.11 = (f32[2,30,32,1]{3,2,1,0:T(8,128)S(1)}, f32[2,30,32,1]{3,2,1,0:T(8,128)}, u32[]{:S(2)}) copy-start(f32[2,30,32,1]{3,2,1,0:T(8,128)} %copy.71) | copy-start | bytes 23044
  68.2 7.9 %copy-start.14 = (f32[2,30,32,1]{3,2,1,0:T(8,128)S(1)}, f32[2,30,32,1]{3,2,1,0:T(8,128)}, u32[]{:S(2)}) copy-start(f32[2,30,32,1]{3,2,1,0:T(8,128)} %copy.69) | copy-start | bytes 23044
  70.1 6.7 %collective-permute-start.10 = (f32[2,30,1,130]{3,2,1,0:T(1,128)S(1)}, f32[2,30,1,130]{3,2,1,0:T(1,128)S(1)}, u32[]{:S(2)}, u32[]{:S(2)}) collective-permute-start(f32[2,30,1,130]{3,2,1,0:T(1,128)S(1)} %get-tuple-element.14), channel_id=1, source_target_pairs={{2,0},{3,1},{6,4},{7,5},{10,8},{11,9},{14,12},{15,13},{18,16},{19,... | collective-permute-start | bytes 93608 | tf_op jit(solution)/shard_map/ppermute | solution.py:19
  71.4 6.6 %copy-start.18 = (f32[30,33,128]{2,1,0:T(8,128)S(1)}, f32[30,33,128]{2,1,0:T(8,128)}, u32[]{:S(2)}) copy-start(f32[30,33,128]{2,1,0:T(8,128)} %copy-done.17) | copy-start | bytes 1520644
  71.4 6.5 %copy-start.22 = (f32[30,33,128]{2,1,0:T(8,128)S(1)}, f32[30,33,128]{2,1,0:T(8,128)}, u32[]{:S(2)}) copy-start(f32[30,33,128]{2,1,0:T(8,128)} %copy-done.21) | copy-start | bytes 1520644
  71.4 6.5 %collective-permute-start.9 = (f32[2,30,1,130]{3,2,1,0:T(1,128)S(1)}, f32[2,30,1,130]{3,2,1,0:T(1,128)S(1)}, u32[]{:S(2)}, u32[]{:S(2)}) collective-permute-start(f32[2,30,1,130]{3,2,1,0:T(1,128)S(1)} %get-tuple-element.13), channel_id=1, source_target_pairs={{0,2},{1,3},{4,6},{5,7},{8,10},{9,11},{12,14},{13,15},{16,18},{17,... | collective-permute-start | bytes 93608 | tf_op jit(solution)/shard_map/ppermute | solution.py:17
  82.1 3.9 %collective-permute-start.12 = (f32[2,30,32,1]{2,1,3,0:T(8,128)S(1)}, f32[2,30,32,1]{2,1,3,0:T(8,128)S(1)}, u32[]{:S(2)}, u32[]{:S(2)}) collective-permute-start(f32[2,30,32,1]{2,1,3,0:T(8,128)S(1)} %copy.76), channel_id=1, source_target_pairs={{4,0},{8,4},{12,8},{0,12},{5,1},{9,5},{13,9},{1,13},{6,2},{10,6},{... | collective-permute-start | bytes 23048 | tf_op jit(solution)/shard_map/ppermute | solution.py:19
  83.3 6.0 %collective-permute-start.11 = (f32[2,30,32,1]{2,1,3,0:T(8,128)}, f32[2,30,32,1]{2,1,3,0:T(8,128)}, u32[]{:S(2)}, u32[]{:S(2)}) collective-permute-start(f32[2,30,32,1]{2,1,3,0:T(8,128)} %copy.74), channel_id=1, source_target_pairs={{0,4},{4,8},{8,12},{12,0},{1,5},{5,9},{9,13},{13,1},{2,6},{6,10},{... | collective-permute-start | bytes 23048 | tf_op jit(solution)/shard_map/ppermute | solution.py:17
  87.5 12.1 %copy-start.5 = (f32[30,32,129]{2,1,0:T(8,128)S(1)}, f32[30,32,129]{2,1,0:T(8,128)}, u32[]{:S(2)}) copy-start(f32[30,32,129]{2,1,0:T(8,128)} %get-tuple-element.18) | copy-start | bytes 1486084
  91.5 8.1 %copy-start.12 = (f32[2,30,32,1]{3,2,1,0:T(8,128)S(1)}, f32[2,30,32,1]{3,2,1,0:T(8,128)}, u32[]{:S(2)}) copy-start(f32[2,30,32,1]{3,2,1,0:T(8,128)} %copy.77) | copy-start | bytes 23044
  91.5 8.1 %copy-start.15 = (f32[2,30,32,1]{3,2,1,0:T(8,128)S(1)}, f32[2,30,32,1]{3,2,1,0:T(8,128)}, u32[]{:S(2)}) copy-start(f32[2,30,32,1]{3,2,1,0:T(8,128)} %copy.75) | copy-start | bytes 23044
  93.4 6.9 %collective-permute-start.14 = (f32[2,30,1,130]{3,2,1,0:T(1,128)S(1)}, f32[2,30,1,130]{3,2,1,0:T(1,128)S(1)}, u32[]{:S(2)}, u32[]{:S(2)}) collective-permute-start(f32[2,30,1,130]{3,2,1,0:T(1,128)S(1)} %get-tuple-element.12), channel_id=1, source_target_pairs={{2,0},{3,1},{6,4},{7,5},{10,8},{11,9},{14,12},{15,13},{18,16},{19,... | collective-permute-start | bytes 93608 | tf_op jit(solution)/shard_map/ppermute | solution.py:19
  94.7 6.6 %copy-start.19 = (f32[30,33,128]{2,1,0:T(8,128)S(1)}, f32[30,33,128]{2,1,0:T(8,128)}, u32[]{:S(2)}) copy-start(f32[30,33,128]{2,1,0:T(8,128)} %copy-done.17) | copy-start | bytes 1520644
  94.7 6.5 %copy-start.23 = (f32[30,33,128]{2,1,0:T(8,128)S(1)}, f32[30,33,128]{2,1,0:T(8,128)}, u32[]{:S(2)}) copy-start(f32[30,33,128]{2,1,0:T(8,128)} %copy-done.21) | copy-start | bytes 1520644
  94.7 6.5 %collective-permute-start.13 = (f32[2,30,1,130]{3,2,1,0:T(1,128)S(1)}, f32[2,30,1,130]{3,2,1,0:T(1,128)S(1)}, u32[]{:S(2)}, u32[]{:S(2)}) collective-permute-start(f32[2,30,1,130]{3,2,1,0:T(1,128)S(1)} %get-tuple-element.11), channel_id=1, source_target_pairs={{0,2},{1,3},{4,6},{5,7},{8,10},{9,11},{12,14},{13,15},{16,18},{17,... | collective-permute-start | bytes 93608 | tf_op jit(solution)/shard_map/ppermute | solution.py:17
  105.5 3.9 %collective-permute-start.16 = (f32[2,30,32,1]{2,1,3,0:T(8,128)S(1)}, f32[2,30,32,1]{2,1,3,0:T(8,128)S(1)}, u32[]{:S(2)}, u32[]{:S(2)}) collective-permute-start(f32[2,30,32,1]{2,1,3,0:T(8,128)S(1)} %copy.82), channel_id=1, source_target_pairs={{4,0},{8,4},{12,8},{0,12},{5,1},{9,5},{13,9},{1,13},{6,2},{10,6},{... | collective-permute-start | bytes 23048 | tf_op jit(solution)/shard_map/ppermute | solution.py:19
  106.7 6.0 %collective-permute-start.15 = (f32[2,30,32,1]{2,1,3,0:T(8,128)}, f32[2,30,32,1]{2,1,3,0:T(8,128)}, u32[]{:S(2)}, u32[]{:S(2)}) collective-permute-start(f32[2,30,32,1]{2,1,3,0:T(8,128)} %copy.80), channel_id=1, source_target_pairs={{0,4},{4,8},{8,12},{12,0},{1,5},{5,9},{9,13},{13,1},{2,6},{6,10},{... | collective-permute-start | bytes 23048 | tf_op jit(solution)/shard_map/ppermute | solution.py:17
  110.8 11.9 %copy-start.6 = (f32[30,32,129]{2,1,0:T(8,128)S(1)}, f32[30,32,129]{2,1,0:T(8,128)}, u32[]{:S(2)}) copy-start(f32[30,32,129]{2,1,0:T(8,128)} %get-tuple-element.18) | copy-start | bytes 1486084
  114.8 7.9 %copy-start.10 = (f32[2,30,32,1]{3,2,1,0:T(8,128)S(1)}, f32[2,30,32,1]{3,2,1,0:T(8,128)}, u32[]{:S(2)}) copy-start(f32[2,30,32,1]{3,2,1,0:T(8,128)} %copy.83) | copy-start | bytes 23044
  114.8 7.9 %copy-start.13 = (f32[2,30,32,1]{3,2,1,0:T(8,128)S(1)}, f32[2,30,32,1]{3,2,1,0:T(8,128)}, u32[]{:S(2)}) copy-start(f32[2,30,32,1]{3,2,1,0:T(8,128)} %copy.81) | copy-start | bytes 23044
  116.7 6.7 %collective-permute-start.18 = (f32[2,30,1,130]{3,2,1,0:T(1,128)S(1)}, f32[2,30,1,130]{3,2,1,0:T(1,128)S(1)}, u32[]{:S(2)}, u32[]{:S(2)}) collective-permute-start(f32[2,30,1,130]{3,2,1,0:T(1,128)S(1)} %get-tuple-element.10), channel_id=1, source_target_pairs={{2,0},{3,1},{6,4},{7,5},{10,8},{11,9},{14,12},{15,13},{18,16},{19,... | collective-permute-start | bytes 93608 | tf_op jit(solution)/shard_map/ppermute | solution.py:19
  118.0 6.6 %copy-start.20 = (f32[30,33,128]{2,1,0:T(8,128)S(1)}, f32[30,33,128]{2,1,0:T(8,128)}, u32[]{:S(2)}) copy-start(f32[30,33,128]{2,1,0:T(8,128)} %copy-done.17) | copy-start | bytes 1520644
  118.0 6.5 %copy-start.24 = (f32[30,33,128]{2,1,0:T(8,128)S(1)}, f32[30,33,128]{2,1,0:T(8,128)}, u32[]{:S(2)}) copy-start(f32[30,33,128]{2,1,0:T(8,128)} %copy-done.21) | copy-start | bytes 1520644
  118.1 6.5 %collective-permute-start.17 = (f32[2,30,1,130]{3,2,1,0:T(1,128)S(1)}, f32[2,30,1,130]{3,2,1,0:T(1,128)S(1)}, u32[]{:S(2)}, u32[]{:S(2)}) collective-permute-start(f32[2,30,1,130]{3,2,1,0:T(1,128)S(1)} %get-tuple-element.9), channel_id=1, source_target_pairs={{0,2},{1,3},{4,6},{5,7},{8,10},{9,11},{12,14},{13,15},{16,18},{17,... | collective-permute-start | bytes 93608 | tf_op jit(solution)/shard_map/ppermute | solution.py:17
  126.8 14.3 %collective-permute-start.20 = (bf16[2,30,32,1]{3,2,1,0:T(8,128)(2,1)}, bf16[2,30,32,1]{3,2,1,0:T(8,128)(2,1)S(1)}, u32[]{:S(2)}, u32[]{:S(2)}) collective-permute-start(bf16[2,30,32,1]{3,2,1,0:T(8,128)(2,1)} %get-tuple-element.34), channel_id=1, source_target_pairs={{4,0},{8,4},{12,8},{0,12},{5,1},{9,5},{13,9},{1,13},{6,2},{10,6},{... | collective-permute-start | bytes 11528 | tf_op jit(solution)/shard_map/ppermute | solution.py:19
  126.9 14.2 %collective-permute-start.19 = (bf16[2,30,32,1]{3,2,1,0:T(8,128)(2,1)S(1)}, bf16[2,30,32,1]{3,2,1,0:T(8,128)(2,1)S(1)}, u32[]{:S(2)}, u32[]{:S(2)}) collective-permute-start(bf16[2,30,32,1]{3,2,1,0:T(8,128)(2,1)S(1)} %get-tuple-element.33), channel_id=1, source_target_pairs={{0,4},{4,8},{8,12},{12,0},{1,5},{5,9},{9,13},{13,1},{2,6},{6,10},{... | collective-permute-start | bytes 11528 | tf_op jit(solution)/shard_map/ppermute | solution.py:17
  131.1 16.5 %copy-start.26 = (bf16[9,2,60,512]{3,2,1,0:T(8,128)(2,1)S(1)}, bf16[9,2,60,512]{3,2,1,0:T(8,128)(2,1)}, u32[]{:S(2)}) copy-start(bf16[9,2,60,512]{3,2,1,0:T(8,128)(2,1)} %reshape.23) | copy-start | bytes 3317764
  141.5 9.1 %collective-permute-start.22 = (bf16[2,30,1,130]{3,2,1,0:T(2,128)(2,1)S(1)}, bf16[2,30,1,130]{3,2,1,0:T(2,128)(2,1)S(1)}, u32[]{:S(2)}, u32[]{:S(2)}) collective-permute-start(bf16[2,30,1,130]{3,2,1,0:T(2,128)(2,1)S(1)} %get-tuple-element.21), channel_id=1, source_target_pairs={{2,0},{3,1},{6,4},{7,5},{10,8},{11,9},{14,12},{15,13},{18,16},{19,... | collective-permute-start | bytes 46808 | tf_op jit(solution)/shard_map/ppermute | solution.py:19
  142.8 7.8 %collective-permute-start.21 = (bf16[2,30,1,130]{3,2,1,0:T(2,128)(2,1)S(1)}, bf16[2,30,1,130]{3,2,1,0:T(2,128)(2,1)S(1)}, u32[]{:S(2)}, u32[]{:S(2)}) collective-permute-start(bf16[2,30,1,130]{3,2,1,0:T(2,128)(2,1)S(1)} %get-tuple-element.22), channel_id=1, source_target_pairs={{0,2},{1,3},{4,6},{5,7},{8,10},{9,11},{12,14},{13,15},{16,18},{17,... | collective-permute-start | bytes 46808 | tf_op jit(solution)/shard_map/ppermute | solution.py:17
  155.8 4.5 %copy-start.27 = (bf16[540,512]{1,0:T(8,128)(2,1)S(1)}, bf16[540,512]{1,0:T(8,128)(2,1)}, u32[]{:S(2)}) copy-start(bf16[540,512]{1,0:T(8,128)(2,1)} %reshape.24) | copy-start | bytes 1658884
  167.0 18.8 %copy-start.28 = (bf16[2,512,120]{1,2,0:T(8,128)(2,1)S(1)}, bf16[2,512,120]{1,2,0:T(8,128)(2,1)}, u32[]{:S(2)}) copy-start(bf16[2,512,120]{1,2,0:T(8,128)(2,1)} %param.11) | copy-start | bytes 737284
  (6 other events, 12.9 us)
Sparse Core Ops, SparseCore 0:
  166.4 14.8 reduce-scatter.1
where the time goes:
time: 202 us; the launch traced here: 200 us
  local copies, waits for them, and re-layouts  52.1 us (26%)
  starting transfers between devices  51.4 us (25%)
  waiting for transfers between devices  41.8 us (21%)
  other arithmetic  24.5 us (12%)
  between operations  14 us (7%)
  matrix products  12 us (6%)
  blocking collectives  4.52 us (2%)
    ppermute x11, starting transfers between devices, with_halo(): lax.ppermute(tail, axis, [(i, (i + 1) % count) for i in range(ends)])  30.6 us
    ppermute x12, starting transfers between devices, with_halo(): lax.ppermute(head, axis, [((i + 1) % count, i) for i in range(ends)])  20.9 us
    ppermute x12, waiting for transfers between devices, with_halo(): lax.ppermute(head, axis, [((i + 1) % count, i) for i in range(ends)])  16.3 us
    reduce_scatter x1, waiting for transfers between devices, shards(): lax.psum_scatter(lax.dot_general(features, local_weight, (((0,), (0,)), (...  14.3 us
    unnamed x73, local copies, waits for them, and re-layouts  12.5 us
    slice x9, local copies, waits for them, and re-layouts, with_halo(): lax.slice_in_dim(cells, cells.shape[dim] - width, cells.shape[dim], axis=...  11.1 us
    ppermute x11, waiting for transfers between devices, with_halo(): lax.ppermute(tail, axis, [(i, (i + 1) % count) for i in range(ends)])  11.1 us
    ppermute x5, local copies, waits for them, and re-layouts, with_halo(): lax.ppermute(tail, axis, [(i, (i + 1) % count) for i in range(ends)])  10.7 us
  transfers between devices with their start and end apart: 24, of which 12 were waited for; matrix products, arithmetic and copies ran while one was open for 17% of the time, Pallas kernels for 0%

commit v1 on v0

v1 whole, which is shorter than its diff:
```python
import functools

import jax
import jax.numpy as jnp
from jax import lax
from jax.experimental import pallas as pl
from jax.experimental.pallas import tpu as pltpu
from jax.sharding import PartitionSpec as P

STEPS = 4
DEEP = STEPS + 1
LP = 32
PACK = 16
MESH = pl.DeviceIdType.MESH


def silu(v):
    half = 0.5 * v
    return half + half * jnp.tanh(half)


def advance(src, winds, row, keep):
    lanes = winds.shape[2]
    east = winds[row, 2 * LP : 3 * LP, :]
    south = winds[row, 3 * LP : 4 * LP, :]
    north = winds[row + 1, 3 * LP : 4 * LP, :]
    east_p, east_n = jnp.maximum(east, 0.0), jnp.minimum(east, 0.0)
    south_p, south_n = jnp.maximum(south, 0.0), jnp.minimum(south, 0.0)
    north_p, north_n = jnp.maximum(north, 0.0), jnp.minimum(north, 0.0)
    out = []
    for f in range(2):
        levels = slice(f * LP, (f + 1) * LP)
        here = src[row, levels, :]
        below = src[row - 1, levels, :]
        above = src[row + 1, levels, :]
        flux_x = east_p * pltpu.roll(here, 1, 1) + east_n * here
        flux_s = south_p * below + south_n * here
        flux_n = north_p * here + north_n * above
        new = here - (pltpu.roll(flux_x, lanes - 1, 1) - flux_x) - (flux_n - flux_s)
        out.append(new * keep)
    return out


def kernel(
    sizes,
    state_ref, winds_ref, mask_ref, w1_ref, w2_ref, head_ref, out_ref,
    x, y, pack, got, corner, cols, feats, tend, back, w1t, w2t,
    send, recv, tsend, trecv,
):
    levels, rows, lane = sizes
    lon, lat, me = lax.axis_index("lon"), lax.axis_index("lat"), lax.axis_index("lev")
    n_lon, n_lat = lax.axis_size("lon"), lax.axis_size("lat")
    share = rows // 2
    right = {"lon": lax.rem(lon + 1, n_lon)}
    left = {"lon": lax.rem(lon + n_lon - 1, n_lon)}
    north, south = {"lat": lat + 1}, {"lat": lat - 1}
    partner = {"lev": 1 - me}
    has_north, has_south = lat < n_lat - 1, lat > 0

    barrier = pltpu.get_barrier_semaphore()
    for other in (right, left, partner):
        pl.semaphore_signal(barrier, inc=1, device_id=other, device_id_type=MESH)

    @pl.when(has_north)
    def _():
        pl.semaphore_signal(barrier, inc=1, device_id=north, device_id_type=MESH)

    @pl.when(has_south)
    def _():
        pl.semaphore_signal(barrier, inc=1, device_id=south, device_id_type=MESH)

    group = lax.broadcasted_iota(jnp.int32, (4 * LP, lane), 1) // 8

    def fill(g, carry):
        eastward = jnp.zeros((4 * LP, lane), jnp.float32)
        westward = jnp.zeros((4 * LP, lane), jnp.float32)
        for k in range(PACK):
            row = g * PACK + k
            pad = jnp.zeros((8, lane), jnp.float32)
            for f in range(2):
                for part, ref in ((0, state_ref), (2, winds_ref)):
                    base = (part + f) * LP
                    x[DEEP + row, base + LP - 8 : base + LP, 0:lane] = pad
                    x[DEEP + row, base : base + levels, 0:lane] = ref[
                        f, pl.ds(row, levels, stride=rows), :
                    ]
            tile = x[DEEP + row, :, 0:lane]
            eastward = jnp.where(group == k, pltpu.roll(tile, (k * 8 + 8) % lane, 1), eastward)
            westward = jnp.where(group == k, pltpu.roll(tile, k * 8, 1), westward)
        pack[0, g] = eastward
        pack[1, g] = westward
        return carry

    lax.fori_loop(0, rows // PACK, fill, 0)

    peers = 3 + jnp.where(has_north, 1, 0) + jnp.where(has_south, 1, 0)
    pl.semaphore_wait(barrier, peers)

    def remote(src, dst, k, device):
        return pltpu.make_async_remote_copy(
            src_ref=src, dst_ref=dst, send_sem=send.at[k], recv_sem=recv.at[k],
            device_id=device, device_id_type=MESH,
        )

    to_right = remote(pack.at[0], got.at[0], 0, right)
    to_left = remote(pack.at[1], got.at[1], 1, left)
    low, high = pl.ds(0, DEEP), pl.ds(DEEP + rows, DEEP)
    inner = pl.ds(0, lane)
    to_south = remote(
        x.at[pl.ds(DEEP, DEEP), :, inner], x.at[high, :, inner], 2, south
    )
    to_north = remote(
        x.at[pl.ds(rows, DEEP), :, inner], x.at[low, :, inner], 3, north
    )
    corner_south = remote(got.at[:, 0], corner.at[1], 4, south)
    corner_north = remote(got.at[:, rows // PACK - 1], corner.at[0], 5, north)

    to_right.start()
    to_left.start()

    @pl.when(has_south)
    def _():
        to_south.start()

    @pl.when(has_north)
    def _():
        to_north.start()

    ghost = jnp.zeros((DEEP,) + x.shape[1:], jnp.float32)

    @pl.when(jnp.logical_not(has_south))
    def _():
        x[0:DEEP] = ghost

    @pl.when(jnp.logical_not(has_north))
    def _():
        x[DEEP + rows : 2 * DEEP + rows] = ghost

    w1t[...] = w1_ref[...].T
    w2t[...] = w2_ref[...].T

    to_right.wait_recv()
    to_left.wait_recv()

    @pl.when(has_south)
    def _():
        corner_south.start()

    @pl.when(has_north)
    def _():
        corner_north.start()

    near = lax.broadcasted_iota(jnp.int32, (4 * LP, lane), 1) < lane // 2

    def beside(from_left, from_right, k):
        return jnp.where(
            near,
            pltpu.roll(from_right, (lane - k * 8) % lane, 1),
            pltpu.roll(from_left, (2 * lane - 8 - k * 8) % lane, 1),
        )

    def unpack(g, carry):
        for k in range(PACK):
            x[DEEP + g * PACK + k, :, lane : 2 * lane] = beside(got[0, g], got[1, g], k)
        return carry

    lax.fori_loop(0, rows // PACK, unpack, 0)

    @pl.when(has_south)
    def _():
        to_north.wait_recv()
        corner_north.wait_recv()
        for k in range(DEEP):
            x[k, :, lane : 2 * lane] = beside(corner[0, 0], corner[0, 1], PACK - DEEP + k)

    @pl.when(has_north)
    def _():
        to_south.wait_recv()
        corner_south.wait_recv()
        for k in range(DEEP):
            x[DEEP + rows + k, :, lane : 2 * lane] = beside(corner[1, 0], corner[1, 1], k)

    to_right.wait_send()
    to_left.wait_send()

    @pl.when(has_south)
    def _():
        to_south.wait_send()
        corner_south.wait_send()

    @pl.when(has_north)
    def _():
        to_north.wait_send()
        corner_north.wait_send()

    keep_south = jnp.where(has_south, 1.0, 0.0)
    keep_north = jnp.where(has_north, 1.0, 0.0)

    def keep(row):
        return jnp.where(
            row < DEEP, keep_south, jnp.where(row >= DEEP + rows, keep_north, 1.0)
        )

    def substep(src, dst, s):
        def body(row, carry):
            new = advance(src, x, row, keep(row))
            for f in range(2):
                dst[row, f * LP : (f + 1) * LP, :] = new[f]
            return carry

        lax.fori_loop(1 + s, 2 * DEEP + rows - 1 - s, body, 0)

    substep(x, y, 0)
    substep(y, x, 1)
    substep(x, y, 2)

    def last(row, carry):
        new = advance(y, x, row, keep(row))
        for f in range(2):
            at = slice(f * LP, (f + 1) * LP)
            x[row, at, 0:lane] = new[f][:, 0:lane]
            k = row - (DEEP - 1)
            cols[k, 0, at, :] = pltpu.roll(new[f], 1, 1)[:, 0:lane].astype(jnp.bfloat16)
            cols[k, 1, at, :] = new[f][:, 0:lane].astype(jnp.bfloat16)
            cols[k, 2, at, :] = pltpu.roll(new[f], 2 * lane - 1, 1)[:, 0:lane].astype(jnp.bfloat16)
        return carry

    lax.fori_loop(DEEP - 1, DEEP + rows + 1, last, 0)

    mine = pl.ds(me * share, share + 2)
    theirs = pl.ds((1 - me) * share, share + 2)
    half = pl.ds(me * 2 * LP, 2 * LP)
    over = remote(cols.at[theirs], feats.at[:, :, half], 6, partner)
    over.start()
    own = pltpu.make_async_copy(cols.at[mine], feats.at[:, :, half], send.at[7])
    own.start()
    own.wait()
    over.wait_recv()

    batch = 4
    steps = share // batch

    def returned(g):
        return pltpu.make_async_remote_copy(
            src_ref=tend.at[pl.ds(g * batch, batch), pl.ds((1 - me) * 2 * LP, 2 * LP)],
            dst_ref=back.at[pl.ds(g * batch, batch)],
            send_sem=tsend.at[g], recv_sem=trecv.at[g], device_id=partner, device_id_type=MESH,
        )

    def emit(row, tendency):
        for f in range(2):
            at = slice(f * LP, f * LP + levels)
            out_ref[f, pl.ds(row, levels, stride=rows), :] = (
                x[DEEP + row, at, 0:lane] + tendency[at]
            )

    def physics(g, carry):
        features = jnp.concatenate(
            [
                feats[pl.ds(g * batch + k, 3)].reshape(9 * 4 * LP, lane)
                for k in range(batch)
            ],
            axis=1,
        )
        first = silu(
            jnp.dot(w1t[...], features, preferred_element_type=jnp.float32)
        ).astype(jnp.bfloat16)
        second = silu(
            jnp.dot(w2t[...], first, preferred_element_type=jnp.float32)
        ).astype(jnp.bfloat16)
        both = jnp.dot(head_ref[...], second, preferred_element_type=jnp.float32)
        for k in range(batch):
            row = g * batch + k
            land = mask_ref[pl.ds(me * share + row, 1), :] == 1
            at = slice(k * lane, (k + 1) * lane)
            tend[row] = jnp.where(land, both[4 * LP :, at], both[: 4 * LP, at])
        returned(g).start()
        for k in range(batch):
            row = g * batch + k
            emit(me * share + row, tend[row, half])
        return carry

    lax.fori_loop(0, steps, physics, 0)

    def finish(g, carry):
        returned(g).wait_recv()
        for k in range(batch):
            row = g * batch + k
            emit((1 - me) * share + row, back[row])
        return carry

    lax.fori_loop(0, steps, finish, 0)
    over.wait_send()

    def drain(g, carry):
        returned(g).wait_send()
        return carry

    lax.fori_loop(0, steps, drain, 0)


def shards(state, winds, land_mask, first_weight, second_weight, head_weight):
    fields, levels, rows, lane = state.shape
    width = second_weight.shape[0]
    lev = lax.axis_size("lev")
    spare = LP - levels
    w1 = first_weight.reshape(9, fields, lev, levels, width).transpose(0, 2, 1, 3, 4)
    w1 = jnp.pad(w1, ((0, 0),) * 3 + ((0, spare), (0, 0))).reshape(-1, width)
    head = head_weight.transpose(0, 2, 1).reshape(2, fields, lev, levels, width)
    head = head.transpose(0, 2, 1, 3, 4)
    head = jnp.pad(head, ((0, 0),) * 3 + ((0, spare), (0, 0))).reshape(-1, width)
    inside = pl.BlockSpec(memory_space=pltpu.VMEM)
    f32, bf16 = jnp.float32, jnp.bfloat16
    groups = rows // PACK
    share = rows // 2
    out = pl.pallas_call(
        functools.partial(kernel, (levels, rows, lane)),
        out_shape=jax.ShapeDtypeStruct((fields, levels * rows, lane), f32),
        in_specs=[inside] * 6,
        out_specs=inside,
        scratch_shapes=[
            pltpu.VMEM((rows + 2 * DEEP, 4 * LP, 2 * lane), f32),
            pltpu.VMEM((rows + 2 * DEEP, 2 * LP, 2 * lane), f32),
            pltpu.VMEM((2, groups, 4 * LP, lane), f32),
            pltpu.VMEM((2, groups, 4 * LP, lane), f32),
            pltpu.VMEM((2, 2, 4 * LP, lane), f32),
            pltpu.VMEM((rows + 2, 3, 2 * LP, lane), bf16),
            pltpu.VMEM((share + 2, 3, 4 * LP, lane), bf16),
            pltpu.VMEM((share, 4 * LP, lane), f32),
            pltpu.VMEM((share, 2 * LP, lane), f32),
            pltpu.VMEM((width, 9 * 4 * LP), bf16),
            pltpu.VMEM((width, width), bf16),
            pltpu.SemaphoreType.DMA((8,)),
            pltpu.SemaphoreType.DMA((8,)),
            pltpu.SemaphoreType.DMA((share // 4,)),
            pltpu.SemaphoreType.DMA((share // 4,)),
        ],
        compiler_params=pltpu.CompilerParams(
            collective_id=0, has_side_effects=True, vmem_limit_bytes=48 * 1024 * 1024
        ),
    )(
        state.reshape(fields, levels * rows, lane),
        winds.reshape(2, levels * rows, lane),
        land_mask,
        w1,
        second_weight,
        head,
    )
    return out.reshape(state.shape)


def solution(mesh):
    placed = (
        P("groups", "lev", "lat", "lon"),
        P("groups", "lev", "lat", "lon"),
        P(("groups", "lat"), "lon"),
        P(),
        P(),
        P(),
    )
    return jax.shard_map(
        shards,
        mesh=mesh,
        in_specs=placed,
        out_specs=P("groups", "lev", "lat", "lon"),
        check_vma=False,
    )
```

time: 202 us -> 58.5 us (0.29)
  Pallas kernels: 0 us -> 54.1 us
  starting transfers between devices: 51.4 us -> 0 us
  local copies, waits for them, and re-layouts: 52.1 us -> 4.16 us
  waiting for transfers between devices: 41.8 us -> 0 us
  other arithmetic: 24.5 us -> 0 us
  between operations: 14 us -> 0.09 us
  matrix products: 12 us -> 0 us
  blocking collectives: 4.52 us -> 0 us
    pallas_call x0 -> x1, Pallas kernels: none -> 54.1 us  [shards(): pl.pallas_call(functools.partial(kernel, (levels, rows, lane)), out_shape...]
    ppermute x23 -> x0, starting transfers between devices: 51.4 us -> none  [the longest x11 30.6 us: with_halo(): lax.ppermute(tail, axis, [(i, (i + 1) % count) for i in range(ends)])]
    ppermute x23 -> x0, waiting for transfers between devices: 27.4 us -> none  [the longest x12 16.3 us: with_halo(): lax.ppermute(head, axis, [((i + 1) % count, i) for i in range(ends)])]
    ppermute x10 -> x0, local copies, waits for them, and re-layouts: 17.5 us -> none  [the longest x5 10.7 us: with_halo(): lax.ppermute(tail, axis, [(i, (i + 1) % count) for i in range(ends)])]
    slice x12 -> x0, local copies, waits for them, and re-layouts: 16 us -> none  [the longest x9 11.1 us: with_halo(): lax.slice_in_dim(cells, cells.shape[dim] - width, cells.shape[dim], axis=...]
    reduce_scatter x1 -> x0, waiting for transfers between devices: 14.3 us -> none  [shards(): lax.psum_scatter(lax.dot_general(features, local_weight, (((0,), (0,)), (...]
    dot_general x4 -> x0, matrix products: 12 us -> none  [the longest x1 6.01 us: shards(): lax.dot_general(features, local_weight, (((0,), (0,)), ((), ())), preferr...]
    unnamed x73 -> x13, local copies, waits for them, and re-layouts: 12.5 us -> 2.42 us
  transfers between devices with their start and end apart: 24 -> 0, of which waited for: 12 -> 0; matrix products, arithmetic and copies ran while one was open for 17% -> 0% of each run, Pallas kernels for 0% -> 0%
where the time goes in v1:
time: 58.5 us; the launch traced here: 58.3 us
  Pallas kernels  54.1 us (92%)
  local copies, waits for them, and re-layouts  4.16 us (7%)
    pallas_call x1, Pallas kernels, shards(): pl.pallas_call(functools.partial(kernel, (levels, rows, lane)), out_shape...  54.1 us
    unnamed x13, local copies, waits for them, and re-layouts  2.42 us
    reshape x1, local copies, waits for them, and re-layouts, shards(): first_weight.reshape(9, fields, lev, levels, width).transpose(0, 2, 1, 3, 4)  1.42 us

profile of v1, /device:TPU:0, one launch (start us, length us, event | category | flops | bytes accessed | tf_op | source)
XLA Modules:
  0.0 58.3 jit_solution(2580159507091613988)
XLA Ops:
  0.0 1.4 %reshape.23 = bf16[9,2,2,30,512]{4,3,2,1,0:T(8,128)(2,1)S(1)} reshape(bf16[1080,512]{1,0:T(8,128)(2,1)} %param.9) | data formatting | bytes 2211840 | tf_op jit(solution)/shard_map/reshape | solution.py:307
  1.4 0.1 copy.12
  1.5 0.0 copy-start.4
  1.5 0.0 copy-start.1
  1.5 0.1 pad.8.clone
  1.7 0.0 copy-start
  1.7 0.0 copy-start.2
  1.7 0.0 copy-start.3
  1.7 0.8 %copy-done.4 = bf16[2,512,120]{1,2,0:T(8,128)(2,1)S(1)} copy-done((bf16[2,512,120]{1,2,0:T(8,128)(2,1)S(1)}, bf16[2,512,120]{1,2,0:T(8,128)(2,1)}, u32[]{:S(2)}) %copy-start.4) | copy-done | bytes 245784
  2.5 0.2 copy.10
  2.7 0.1 copy-done.1
  2.9 0.3 copy-done
  3.2 0.1 copy-done.2
  3.3 0.0 copy-done.3
  3.3 54.1 %shard_map.64 = f32[2,960,128]{2,1,0:T(8,128)S(1)} custom-call(f32[2,960,128]{2,1,0:T(8,128)S(1)} %bitcast.13, f32[2,960,128]{2,1,0:T(8,128)S(1)} %bitcast.14, s32[32,128]{1,0:T(8,128)S(1)} %copy-done.3, bf16[1152,512]{1,0:T(8,128)(2,1)S(1)} %bitcast.10, bf16[512,512]{1,0:T(8,128)(2,1)S(1)} %copy-done.2, bf16[256,512]{1,0:T(8,128)(2,1)S(1)} %bitcast.12), custom_call_target="tpu_custom_call" | custom-call | tf_op jit(solution)/shard_map/pallas_call | solution.py:316
  57.4 0.9 %copy.15 = f32[2,30,32,128]{3,2,1,0:T(8,128)} copy(f32[2,30,32,128]{3,2,1,0:T(8,128)S(1)} %bitcast.11) | data formatting | bytes 1966080
  (2 shorter events, 0.1 us)
Async XLA Ops:
  1.5 0.9 %copy-start.4 = (bf16[2,512,120]{1,2,0:T(8,128)(2,1)S(1)}, bf16[2,512,120]{1,2,0:T(8,128)(2,1)}, u32[]{:S(2)}) copy-start(bf16[2,512,120]{1,2,0:T(8,128)(2,1)} %param.11) | copy-start | bytes 737284
  1.5 1.3 %copy-start.1 = (f32[2,30,32,128]{3,2,1,0:T(8,128)S(1)}, f32[2,30,32,128]{3,2,1,0:T(8,128)}, u32[]{:S(2)}) copy-start(f32[2,30,32,128]{3,2,1,0:T(8,128)} %param.7) | copy-start | bytes 2949124
  1.7 1.5 %copy-start = (f32[2,30,32,128]{3,2,1,0:T(8,128)S(1)}, f32[2,30,32,128]{3,2,1,0:T(8,128)}, u32[]{:S(2)}) copy-start(f32[2,30,32,128]{3,2,1,0:T(8,128)} %param.6) | copy-start | bytes 2949124
  1.7 1.6 %copy-start.2 = (bf16[512,512]{1,0:T(8,128)(2,1)S(1)}, bf16[512,512]{1,0:T(8,128)(2,1)}, u32[]{:S(2)}) copy-start(bf16[512,512]{1,0:T(8,128)(2,1)} %w2_ref.1) | copy-start | bytes 1572868
  1.7 1.6 %copy-start.3 = (s32[32,128]{1,0:T(8,128)S(1)}, s32[32,128]{1,0:T(8,128)}, u32[]{:S(2)}) copy-start(s32[32,128]{1,0:T(8,128)} %mask_ref.1) | copy-start | bytes 49156

commit v2 on v1

v2 whole, which is shorter than its diff:
```python
import functools

import jax
import jax.numpy as jnp
from jax import lax
from jax.experimental import pallas as pl
from jax.experimental.pallas import tpu as pltpu
from jax.sharding import PartitionSpec as P

STEPS = 4
DEEP = STEPS + 1
LP = 32
EDGE = 8
MESH = pl.DeviceIdType.MESH


def silu(v):
    half = 0.5 * v
    return half + half * jnp.tanh(half)


def chunks():
    for c in range(LP // 8):
        yield 8 * c, LP + 8 * c, (8 * c, LP + 8 * c)
    for side in range(2):
        yield 2 * LP + 8 * side, 2 * LP + 16 + 8 * side, (2 * LP + 8 * side,)


def advance(src, winds, row, keeps):
    n = len(keeps)
    for z_at, m_at, tracers in chunks():
        zonal = [winds[row + k, z_at : z_at + 8, :] for k in range(n)]
        merid = [winds[row + k, m_at : m_at + 8, :] for k in range(n + 1)]
        for at in tracers:
            cells = [src[row - 1 + k, at : at + 8, :] for k in range(n + 2)]
            flux_y = [
                merid[k] * jnp.where(merid[k] > 0.0, cells[k], cells[k + 1])
                for k in range(n + 1)
            ]
            for k in range(n):
                here = cells[k + 1]
                lanes = here.shape[1]
                flux_x = zonal[k] * jnp.where(zonal[k] > 0.0, pltpu.roll(here, 1, 1), here)
                new = here - (pltpu.roll(flux_x, lanes - 1, 1) - flux_x)
                new = new - (flux_y[k + 1] - flux_y[k])
                yield k, at, new * keeps[k]


def kernel(
    sizes,
    state_ref, winds_ref, mask_ref, w1_ref, w2_ref, head_ref, out_ref,
    x, y, w, pack, got, cols, feats, tend, back, w1t, w2t,
    send, recv, tsend, trecv,
):
    levels, rows, lane = sizes
    lon, lat, me = lax.axis_index("lon"), lax.axis_index("lat"), lax.axis_index("lev")
    n_lon, n_lat = lax.axis_size("lon"), lax.axis_size("lat")
    share = rows // 2
    right = {"lon": lax.rem(lon + 1, n_lon)}
    left = {"lon": lax.rem(lon + n_lon - 1, n_lon)}
    north, south = {"lat": lat + 1}, {"lat": lat - 1}
    partner = {"lev": 1 - me}
    has_north, has_south = lat < n_lat - 1, lat > 0

    barrier = pltpu.get_barrier_semaphore()
    for other in (right, left, partner):
        pl.semaphore_signal(barrier, inc=1, device_id=other, device_id_type=MESH)

    @pl.when(has_north)
    def _():
        pl.semaphore_signal(barrier, inc=1, device_id=north, device_id_type=MESH)

    @pl.when(has_south)
    def _():
        pl.semaphore_signal(barrier, inc=1, device_id=south, device_id_type=MESH)

    place = lax.broadcasted_iota(jnp.int32, (8, lane), 1)
    group = place // (2 * EDGE)
    first_half = place % (2 * EDGE) < EDGE

    def fill(row, carry):
        pad = jnp.zeros((8, lane), jnp.float32)
        for f in range(2):
            for into, ref in ((x, state_ref), (w, winds_ref)):
                base = f * LP
                into[DEEP + row, base + LP - 8 : base + LP, :] = pad
                into[DEEP + row, base : base + levels, :] = ref[
                    f, pl.ds(row, levels, stride=rows), :
                ]
        for side in range(2):
            begin = lane - EDGE if side == 0 else 0
            halves = []
            for into, half_at in ((x, 0), (w, EDGE)):
                acc = pad
                for c in range(8):
                    tile = into[DEEP + row, 8 * c : 8 * c + 8, :]
                    shift = (c * 2 * EDGE + half_at - begin) % lane
                    moved = pltpu.roll(tile, shift, 1) if shift else tile
                    acc = jnp.where(group == c, moved, acc)
                halves.append(acc)
            pack[side, DEEP + row] = jnp.where(first_half, halves[0], halves[1])
        return carry

    lax.fori_loop(0, rows, fill, 0)

    peers = 3 + jnp.where(has_north, 1, 0) + jnp.where(has_south, 1, 0)
    pl.semaphore_wait(barrier, peers)

    def remote(src, dst, k, device):
        return pltpu.make_async_remote_copy(
            src_ref=src, dst_ref=dst, send_sem=send.at[k], recv_sem=recv.at[k],
            device_id=device, device_id_type=MESH,
        )

    interior = pl.ds(DEEP, rows)
    to_right = remote(pack.at[0, interior], got.at[0, interior], 0, right)
    to_left = remote(pack.at[1, interior], got.at[1, interior], 1, left)
    low, high = pl.ds(0, DEEP), pl.ds(DEEP + rows, DEEP)
    bottom, top = pl.ds(DEEP, DEEP), pl.ds(rows, DEEP)
    main = pl.ds(0, 2 * LP)
    to_south = [
        remote(x.at[bottom, main], x.at[high, main], 2, south),
        remote(w.at[bottom, main], w.at[high, main], 3, south),
        remote(pack.at[:, bottom], pack.at[:, high], 4, south),
    ]
    to_north = [
        remote(x.at[top, main], x.at[low, main], 6, north),
        remote(w.at[top, main], w.at[low, main], 7, north),
        remote(pack.at[:, top], pack.at[:, low], 8, north),
    ]
    corner_south = remote(got.at[:, bottom], got.at[:, high], 5, south)
    corner_north = remote(got.at[:, top], got.at[:, low], 9, north)

    to_right.start()
    to_left.start()

    @pl.when(has_south)
    def _():
        for copy in to_south:
            copy.start()

    @pl.when(has_north)
    def _():
        for copy in to_north:
            copy.start()

    def clear(begin):
        for k in range(DEEP):
            x[begin + k] = jnp.zeros(x.shape[1:], jnp.float32)
            w[begin + k] = jnp.zeros(w.shape[1:], jnp.float32)
            for side in range(2):
                pack[side, begin + k] = jnp.zeros((8, lane), jnp.float32)
                got[side, begin + k] = jnp.zeros((8, lane), jnp.float32)

    @pl.when(jnp.logical_not(has_south))
    def _():
        clear(0)

    @pl.when(jnp.logical_not(has_north))
    def _():
        clear(DEEP + rows)

    w1t[...] = w1_ref[...].T
    w2t[...] = w2_ref[...].T

    to_right.wait_recv()
    to_left.wait_recv()

    @pl.when(has_south)
    def _():
        corner_south.start()

    @pl.when(has_north)
    def _():
        corner_north.start()

    def strips(row, carry):
        for side in range(2):
            if side == 0:
                outer, inner = got[0, row], pack[1, row]
            else:
                outer, inner = pack[0, row], got[1, row]
            tracer = jnp.where(first_half, outer, pltpu.roll(inner, EDGE, 1))
            wind = jnp.where(first_half, pltpu.roll(outer, lane - EDGE, 1), inner)
            swapped = pltpu.roll(wind, lane // 2, 1)
            at = 2 * LP + 8 * side
            x[row, at : at + 8, :] = tracer
            w[row, at : at + 8, :] = jnp.where(place < lane // 2, wind, swapped)
            w[row, at + 16 : at + 24, :] = jnp.where(place < lane // 2, swapped, wind)
        return carry

    lax.fori_loop(DEEP, DEEP + rows, strips, 0)

    @pl.when(has_south)
    def _():
        for copy in to_north:
            copy.wait_recv()
        corner_north.wait_recv()

    @pl.when(has_north)
    def _():
        for copy in to_south:
            copy.wait_recv()
        corner_south.wait_recv()

    lax.fori_loop(0, DEEP, strips, 0)
    lax.fori_loop(DEEP + rows, 2 * DEEP + rows, strips, 0)

    to_right.wait_send()
    to_left.wait_send()

    @pl.when(has_south)
    def _():
        for copy in to_south:
            copy.wait_send()
        corner_south.wait_send()

    @pl.when(has_north)
    def _():
        for copy in to_north:
            copy.wait_send()
        corner_north.wait_send()

    keep_south = jnp.where(has_south, 1.0, 0.0)
    keep_north = jnp.where(has_north, 1.0, 0.0)

    def keep(row):
        return jnp.where(
            row < DEEP, keep_south, jnp.where(row >= DEEP + rows, keep_north, 1.0)
        )

    def substep(src, dst, s):
        first = 1 + s
        count = 2 * DEEP + rows - 2 - 2 * s

        def body(i, carry):
            row = first + 2 * i
            for k, at, new in advance(src, w, row, [keep(row), keep(row + 1)]):
                dst[row + k, at : at + 8, :] = new
            return carry

        lax.fori_loop(0, count // 2, body, 0)

    substep(x, y, 0)
    substep(y, x, 1)
    substep(x, y, 2)
    substep(y, x, 3)

    def merge(k, carry):
        row = k + DEEP - 1
        west = x[row, 2 * LP : 2 * LP + 8, :]
        east = x[row, 2 * LP + 8 : 2 * LP + 16, :]
        for c in range(0, 8, 2):
            shifted = ([], [], [])
            for d in (c, c + 1):
                at = slice(8 * d, 8 * d + 8)
                from_west = pltpu.roll(west, (2 * lane - EDGE - d * 2 * EDGE) % lane, 1)
                shift = (lane - EDGE - d * 2 * EDGE) % lane
                from_east = pltpu.roll(east, shift, 1) if shift else east
                cells = jnp.where(place < STEPS, from_west, x[row, at, :])
                cells = jnp.where(place >= lane - STEPS, from_east, cells)
                x[row, at, :] = cells
                shifted[0].append(
                    pltpu.roll(jnp.where(place == lane - 1, from_west, cells), 1, 1)
                )
                shifted[1].append(cells)
                shifted[2].append(
                    pltpu.roll(jnp.where(place == 0, from_east, cells), lane - 1, 1)
                )
            for b in range(3):
                cols[k, b, 8 * c : 8 * c + 16, :] = jnp.concatenate(shifted[b], 0).astype(
                    jnp.bfloat16
                )
        return carry

    lax.fori_loop(0, rows + 2, merge, 0)

    mine = pl.ds(me * share, share + 2)
    theirs = pl.ds((1 - me) * share, share + 2)
    half = pl.ds(me * 2 * LP, 2 * LP)
    over = remote(cols.at[theirs], feats.at[:, :, half], 10, partner)
    over.start()
    own = pltpu.make_async_copy(cols.at[mine], feats.at[:, :, half], send.at[11])
    own.start()
    own.wait()
    over.wait_recv()

    batch = 4
    steps = share // batch

    def returned(g):
        return pltpu.make_async_remote_copy(
            src_ref=tend.at[pl.ds(g * batch, batch), pl.ds((1 - me) * 2 * LP, 2 * LP)],
            dst_ref=back.at[pl.ds(g * batch, batch)],
            send_sem=tsend.at[g], recv_sem=trecv.at[g], device_id=partner, device_id_type=MESH,
        )

    def emit(row, tendency):
        for f in range(2):
            at = slice(f * LP, f * LP + levels)
            out_ref[f, pl.ds(row, levels, stride=rows), :] = (
                x[DEEP + row, at, :] + tendency[at]
            )

    def physics(g, carry):
        features = jnp.concatenate(
            [
                feats[pl.ds(g * batch + k, 3)].reshape(9 * 4 * LP, lane)
                for k in range(batch)
            ],
            axis=1,
        )
        first = silu(
            jnp.dot(w1t[...], features, preferred_element_type=jnp.float32)
        ).astype(jnp.bfloat16)
        second = silu(
            jnp.dot(w2t[...], first, preferred_element_type=jnp.float32)
        ).astype(jnp.bfloat16)
        both = jnp.dot(head_ref[...], second, preferred_element_type=jnp.float32)
        for k in range(batch):
            row = g * batch + k
            land = mask_ref[pl.ds(me * share + row, 1), :] == 1
            at = slice(k * lane, (k + 1) * lane)
            tend[row] = jnp.where(land, both[4 * LP :, at], both[: 4 * LP, at])
        returned(g).start()
        for k in range(batch):
            row = g * batch + k
            emit(me * share + row, tend[row, half])
        return carry

    lax.fori_loop(0, steps, physics, 0)

    def finish(g, carry):
        returned(g).wait_recv()
        for k in range(batch):
            row = g * batch + k
            emit((1 - me) * share + row, back[row])
        return carry

    lax.fori_loop(0, steps, finish, 0)
    over.wait_send()

    def drain(g, carry):
        returned(g).wait_send()
        return carry

    lax.fori_loop(0, steps, drain, 0)


def shards(state, winds, land_mask, first_weight, second_weight, head_weight):
    fields, levels, rows, lane = state.shape
    width = second_weight.shape[0]
    lev = lax.axis_size("lev")
    spare = LP - levels
    w1 = first_weight.reshape(9, fields, lev, levels, width).transpose(0, 2, 1, 3, 4)
    w1 = jnp.pad(w1, ((0, 0),) * 3 + ((0, spare), (0, 0))).reshape(-1, width)
    head = head_weight.transpose(0, 2, 1).reshape(2, fields, lev, levels, width)
    head = head.transpose(0, 2, 1, 3, 4)
    head = jnp.pad(head, ((0, 0),) * 3 + ((0, spare), (0, 0))).reshape(-1, width)
    inside = pl.BlockSpec(memory_space=pltpu.VMEM)
    f32, bf16 = jnp.float32, jnp.bfloat16
    share = rows // 2
    out = pl.pallas_call(
        functools.partial(kernel, (levels, rows, lane)),
        out_shape=jax.ShapeDtypeStruct((fields, levels * rows, lane), f32),
        in_specs=[inside] * 6,
        out_specs=inside,
        scratch_shapes=[
            pltpu.VMEM((rows + 2 * DEEP, 2 * LP + 16, lane), f32),
            pltpu.VMEM((rows + 2 * DEEP, 2 * LP + 16, lane), f32),
            pltpu.VMEM((rows + 2 * DEEP, 2 * LP + 32, lane), f32),
            pltpu.VMEM((2, rows + 2 * DEEP, 8, lane), f32),
            pltpu.VMEM((2, rows + 2 * DEEP, 8, lane), f32),
            pltpu.VMEM((rows + 2, 3, 2 * LP, lane), bf16),
            pltpu.VMEM((share + 2, 3, 4 * LP, lane), bf16),
            pltpu.VMEM((share, 4 * LP, lane), f32),
            pltpu.VMEM((share, 2 * LP, lane), f32),
            pltpu.VMEM((width, 9 * 4 * LP), bf16),
            pltpu.VMEM((width, width), bf16),
            pltpu.SemaphoreType.DMA((12,)),
            pltpu.SemaphoreType.DMA((12,)),
            pltpu.SemaphoreType.DMA((share // 4,)),
            pltpu.SemaphoreType.DMA((share // 4,)),
        ],
        compiler_params=pltpu.CompilerParams(
            collective_id=0, has_side_effects=True, vmem_limit_bytes=48 * 1024 * 1024
        ),
    )(
        state.reshape(fields, levels * rows, lane),
        winds.reshape(2, levels * rows, lane),
        land_mask,
        w1,
        second_weight,
        head,
    )
    return out.reshape(state.shape)


def solution(mesh):
    placed = (
        P("groups", "lev", "lat", "lon"),
        P("groups", "lev", "lat", "lon"),
        P(("groups", "lat"), "lon"),
        P(),
        P(),
        P(),
    )
    return jax.shard_map(
        shards,
        mesh=mesh,
        in_specs=placed,
        out_specs=P("groups", "lev", "lat", "lon"),
        check_vma=False,
    )
```

time: 58.5 us -> 51.7 us (0.88)
  Pallas kernels: 54.1 us -> 47.3 us
    pallas_call x1, Pallas kernels: 54.1 us -> 47.3 us  [shards(): pl.pallas_call(functools.partial(kernel, (levels, rows, lane)), out_shape...]
where the time goes in v2:
time: 51.7 us; the launch traced here: 51.6 us
  Pallas kernels  47.3 us (91%)
  local copies, waits for them, and re-layouts  4.16 us (8%)
    pallas_call x1, Pallas kernels, shards(): pl.pallas_call(functools.partial(kernel, (levels, rows, lane)), out_shape...  47.3 us
    unnamed x13, local copies, waits for them, and re-layouts  2.42 us
    reshape x1, local copies, waits for them, and re-layouts, shards(): first_weight.reshape(9, fields, lev, levels, width).transpose(0, 2, 1, 3, 4)  1.42 us

profile of v2, /device:TPU:0, one launch (start us, length us, event | category | flops | bytes accessed | tf_op | source)
XLA Modules:
  0.0 51.6 jit_solution(10914389104846139033)
XLA Ops:
  0.0 1.4 %reshape.23 = bf16[9,2,2,30,512]{4,3,2,1,0:T(8,128)(2,1)S(1)} reshape(bf16[1080,512]{1,0:T(8,128)(2,1)} %param.9) | data formatting | bytes 2211840 | tf_op jit(solution)/shard_map/reshape | solution.py:355
  1.4 0.1 copy.12
  1.5 0.0 copy-start.4
  1.5 0.0 copy-start.1
  1.5 0.1 pad.8.clone
  1.7 0.0 copy-start
  1.7 0.0 copy-start.2
  1.7 0.0 copy-start.3
  1.7 0.8 %copy-done.4 = bf16[2,512,120]{1,2,0:T(8,128)(2,1)S(1)} copy-done((bf16[2,512,120]{1,2,0:T(8,128)(2,1)S(1)}, bf16[2,512,120]{1,2,0:T(8,128)(2,1)}, u32[]{:S(2)}) %copy-start.4) | copy-done | bytes 245784
  2.5 0.2 copy.10
  2.7 0.1 copy-done.1
  2.9 0.3 copy-done
  3.2 0.1 copy-done.2
  3.3 0.0 copy-done.3
  3.3 47.3 %shard_map.64 = f32[2,960,128]{2,1,0:T(8,128)S(1)} custom-call(f32[2,960,128]{2,1,0:T(8,128)S(1)} %bitcast.13, f32[2,960,128]{2,1,0:T(8,128)S(1)} %bitcast.14, s32[32,128]{1,0:T(8,128)S(1)} %copy-done.3, bf16[1152,512]{1,0:T(8,128)(2,1)S(1)} %bitcast.10, bf16[512,512]{1,0:T(8,128)(2,1)S(1)} %copy-done.2, bf16[256,512]{1,0:T(8,128)(2,1)S(1)} %bitcast.12), custom_call_target="tpu_custom_call" | custom-call | tf_op jit(solution)/shard_map/pallas_call | solution.py:363
  50.6 0.9 %copy.15 = f32[2,30,32,128]{3,2,1,0:T(8,128)} copy(f32[2,30,32,128]{3,2,1,0:T(8,128)S(1)} %bitcast.11) | data formatting | bytes 1966080
  (2 shorter events, 0.1 us)
Async XLA Ops:
  1.5 0.9 %copy-start.4 = (bf16[2,512,120]{1,2,0:T(8,128)(2,1)S(1)}, bf16[2,512,120]{1,2,0:T(8,128)(2,1)}, u32[]{:S(2)}) copy-start(bf16[2,512,120]{1,2,0:T(8,128)(2,1)} %param.11) | copy-start | bytes 737284
  1.5 1.3 %copy-start.1 = (f32[2,30,32,128]{3,2,1,0:T(8,128)S(1)}, f32[2,30,32,128]{3,2,1,0:T(8,128)}, u32[]{:S(2)}) copy-start(f32[2,30,32,128]{3,2,1,0:T(8,128)} %param.7) | copy-start | bytes 2949124
  1.7 1.5 %copy-start = (f32[2,30,32,128]{3,2,1,0:T(8,128)S(1)}, f32[2,30,32,128]{3,2,1,0:T(8,128)}, u32[]{:S(2)}) copy-start(f32[2,30,32,128]{3,2,1,0:T(8,128)} %param.6) | copy-start | bytes 2949124
  1.7 1.6 %copy-start.2 = (bf16[512,512]{1,0:T(8,128)(2,1)S(1)}, bf16[512,512]{1,0:T(8,128)(2,1)}, u32[]{:S(2)}) copy-start(bf16[512,512]{1,0:T(8,128)(2,1)} %w2_ref.1) | copy-start | bytes 1572868
  1.7 1.6 %copy-start.3 = (s32[32,128]{1,0:T(8,128)S(1)}, s32[32,128]{1,0:T(8,128)}, u32[]{:S(2)}) copy-start(s32[32,128]{1,0:T(8,128)} %mask_ref.1) | copy-start | bytes 49156

commit v3 on v2

--- a/solution.py
+++ b/solution.py
@@ -78,30 +78,38 @@
     group = place // (2 * EDGE)
     first_half = place % (2 * EDGE) < EDGE
 
-    def fill(row, carry):
-        pad = jnp.zeros((8, lane), jnp.float32)
+    def tiles(ref, row):
         for f in range(2):
-            for into, ref in ((x, state_ref), (w, winds_ref)):
-                base = f * LP
-                into[DEEP + row, base + LP - 8 : base + LP, :] = pad
-                into[DEEP + row, base : base + levels, :] = ref[
-                    f, pl.ds(row, levels, stride=rows), :
-                ]
+            for c in range(LP // 8):
+                count = min(8, levels - 8 * c)
+                tile = ref[f, pl.ds(row + 8 * c * rows, count, stride=rows), :]
+                if count < 8:
+                    tile = jnp.concatenate([tile, jnp.zeros((8 - count, lane), jnp.float32)], 0)
+                yield tile
+
+    def fill_row(row):
+        tracers, winds = list(tiles(state_ref, row)), list(tiles(winds_ref, row))
+        for into, values in ((x, tracers), (w, winds)):
+            for c, tile in enumerate(values):
+                into[DEEP + row, 8 * c : 8 * c + 8, :] = tile
         for side in range(2):
             begin = lane - EDGE if side == 0 else 0
             halves = []
-            for into, half_at in ((x, 0), (w, EDGE)):
-                acc = pad
-                for c in range(8):
-                    tile = into[DEEP + row, 8 * c : 8 * c + 8, :]
+            for values, half_at in ((tracers, 0), (winds, EDGE)):
+                acc = jnp.zeros((8, lane), jnp.float32)
+                for c, tile in enumerate(values):
                     shift = (c * 2 * EDGE + half_at - begin) % lane
                     moved = pltpu.roll(tile, shift, 1) if shift else tile
                     acc = jnp.where(group == c, moved, acc)
                 halves.append(acc)
             pack[side, DEEP + row] = jnp.where(first_half, halves[0], halves[1])
-        return carry
-
-    lax.fori_loop(0, rows, fill, 0)
+
+    def fill(i, carry):
+        fill_row(2 * i)
+        fill_row(2 * i + 1)
+        return carry
+
+    lax.fori_loop(0, rows // 2, fill, 0)
 
     peers = 3 + jnp.where(has_north, 1, 0) + jnp.where(has_south, 1, 0)
     pl.semaphore_wait(barrier, peers)
@@ -189,7 +197,12 @@
             w[row, at + 16 : at + 24, :] = jnp.where(place < lane // 2, swapped, wind)
         return carry
 
-    lax.fori_loop(DEEP, DEEP + rows, strips, 0)
+    def strips_four(i, carry):
+        for k in range(4):
+            strips(DEEP + 4 * i + k, carry)
+        return carry
+
+    lax.fori_loop(0, rows // 4, strips_four, 0)
 
     @pl.when(has_south)
     def _():
@@ -203,8 +216,12 @@
             copy.wait_recv()
         corner_south.wait_recv()
 
-    lax.fori_loop(0, DEEP, strips, 0)
-    lax.fori_loop(DEEP + rows, 2 * DEEP + rows, strips, 0)
+    def strips_ends(k, carry):
+        strips(k, carry)
+        strips(DEEP + rows + k, carry)
+        return carry
+
+    lax.fori_loop(0, DEEP, strips_ends, 0)
 
     to_right.wait_send()
     to_left.wait_send()
@@ -230,23 +247,23 @@
         )
 
     def substep(src, dst, s):
-        first = 1 + s
-        count = 2 * DEEP + rows - 2 - 2 * s
+        first = 1 + s // 2 * 2
+        count = 2 * DEEP + rows + 1 - 2 * first - 1
 
         def body(i, carry):
-            row = first + 2 * i
-            for k, at, new in advance(src, w, row, [keep(row), keep(row + 1)]):
+            row = first + 4 * i
+            for k, at, new in advance(src, w, row, [keep(row + k) for k in range(4)]):
                 dst[row + k, at : at + 8, :] = new
             return carry
 
-        lax.fori_loop(0, count // 2, body, 0)
+        lax.fori_loop(0, count // 4, body, 0)
 
     substep(x, y, 0)
     substep(y, x, 1)
     substep(x, y, 2)
     substep(y, x, 3)
 
-    def merge(k, carry):
+    def merge_row(k):
         row = k + DEEP - 1
         west = x[row, 2 * LP : 2 * LP + 8, :]
         east = x[row, 2 * LP + 8 : 2 * LP + 16, :]
@@ -259,7 +276,7 @@
                 from_east = pltpu.roll(east, shift, 1) if shift else east
                 cells = jnp.where(place < STEPS, from_west, x[row, at, :])
                 cells = jnp.where(place >= lane - STEPS, from_east, cells)
-                x[row, at, :] = cells
+                y[row, at, :] = cells
                 shifted[0].append(
                     pltpu.roll(jnp.where(place == lane - 1, from_west, cells), 1, 1)
                 )
@@ -271,15 +288,22 @@
                 cols[k, b, 8 * c : 8 * c + 16, :] = jnp.concatenate(shifted[b], 0).astype(
                     jnp.bfloat16
                 )
-        return carry
-
-    lax.fori_loop(0, rows + 2, merge, 0)
+
+    def merge_from(start, count):
+        def body(i, carry):
+            merge_row(start + 2 * i)
+            merge_row(start + 2 * i + 1)
+            return carry
+
+        lax.fori_loop(0, count // 2, body, 0)
 
     mine = pl.ds(me * share, share + 2)
     theirs = pl.ds((1 - me) * share, share + 2)
     half = pl.ds(me * 2 * LP, 2 * LP)
     over = remote(cols.at[theirs], feats.at[:, :, half], 10, partner)
+    merge_from((1 - me) * share, share + 2)
     over.start()
+    merge_from(me * (share + 2), share)
     own = pltpu.make_async_copy(cols.at[mine], feats.at[:, :, half], send.at[11])
     own.start()
     own.wait()
@@ -299,7 +323,7 @@
         for f in range(2):
             at = slice(f * LP, f * LP + levels)
             out_ref[f, pl.ds(row, levels, stride=rows), :] = (
-                x[DEEP + row, at, :] + tendency[at]
+                y[DEEP + row, at, :] + tendency[at]
             )
 
     def physics(g, carry):

time: 51.7 us -> 39.8 us (0.77)
  Pallas kernels: 47.3 us -> 35.4 us
    pallas_call x1, Pallas kernels: 47.3 us -> 35.4 us  [shards(): pl.pallas_call(functools.partial(kernel, (levels, rows, lane)), out_shape...]
where the time goes in v3:
time: 39.8 us; the launch traced here: 39.6 us
  Pallas kernels  35.4 us (89%)
  local copies, waits for them, and re-layouts  4.16 us (10%)
    pallas_call x1, Pallas kernels, shards(): pl.pallas_call(functools.partial(kernel, (levels, rows, lane)), out_shape...  35.4 us
    unnamed x13, local copies, waits for them, and re-layouts  2.42 us
    reshape x1, local copies, waits for them, and re-layouts, shards(): first_weight.reshape(9, fields, lev, levels, width).transpose(0, 2, 1, 3, 4)  1.42 us

profile of v3, /device:TPU:0, one launch (start us, length us, event | category | flops | bytes accessed | tf_op | source)
XLA Modules:
  0.0 39.6 jit_solution(14011556700380030857)
XLA Ops:
  0.0 1.4 %reshape.23 = bf16[9,2,2,30,512]{4,3,2,1,0:T(8,128)(2,1)S(1)} reshape(bf16[1080,512]{1,0:T(8,128)(2,1)} %param.9) | data formatting | bytes 2211840 | tf_op jit(solution)/shard_map/reshape | solution.py:379
  1.4 0.1 copy.12
  1.5 0.0 copy-start.4
  1.5 0.0 copy-start.1
  1.5 0.1 pad.8.clone
  1.7 0.0 copy-start
  1.7 0.0 copy-start.2
  1.7 0.0 copy-start.3
  1.7 0.8 %copy-done.4 = bf16[2,512,120]{1,2,0:T(8,128)(2,1)S(1)} copy-done((bf16[2,512,120]{1,2,0:T(8,128)(2,1)S(1)}, bf16[2,512,120]{1,2,0:T(8,128)(2,1)}, u32[]{:S(2)}) %copy-start.4) | copy-done | bytes 245784
  2.5 0.2 copy.10
  2.7 0.1 copy-done.1
  2.9 0.3 copy-done
  3.2 0.1 copy-done.2
  3.3 0.0 copy-done.3
  3.3 35.4 %shard_map.64 = f32[2,960,128]{2,1,0:T(8,128)S(1)} custom-call(f32[2,960,128]{2,1,0:T(8,128)S(1)} %bitcast.13, f32[2,960,128]{2,1,0:T(8,128)S(1)} %bitcast.14, s32[32,128]{1,0:T(8,128)S(1)} %copy-done.3, bf16[1152,512]{1,0:T(8,128)(2,1)S(1)} %bitcast.10, bf16[512,512]{1,0:T(8,128)(2,1)S(1)} %copy-done.2, bf16[256,512]{1,0:T(8,128)(2,1)S(1)} %bitcast.12), custom_call_target="tpu_custom_call" | custom-call | tf_op jit(solution)/shard_map/pallas_call | solution.py:387
  38.7 0.9 %copy.15 = f32[2,30,32,128]{3,2,1,0:T(8,128)} copy(f32[2,30,32,128]{3,2,1,0:T(8,128)S(1)} %bitcast.11) | data formatting | bytes 1966080
  (2 shorter events, 0.1 us)
Async XLA Ops:
  1.5 0.9 %copy-start.4 = (bf16[2,512,120]{1,2,0:T(8,128)(2,1)S(1)}, bf16[2,512,120]{1,2,0:T(8,128)(2,1)}, u32[]{:S(2)}) copy-start(bf16[2,512,120]{1,2,0:T(8,128)(2,1)} %param.11) | copy-start | bytes 737284
  1.5 1.3 %copy-start.1 = (f32[2,30,32,128]{3,2,1,0:T(8,128)S(1)}, f32[2,30,32,128]{3,2,1,0:T(8,128)}, u32[]{:S(2)}) copy-start(f32[2,30,32,128]{3,2,1,0:T(8,128)} %param.7) | copy-start | bytes 2949124
  1.7 1.5 %copy-start = (f32[2,30,32,128]{3,2,1,0:T(8,128)S(1)}, f32[2,30,32,128]{3,2,1,0:T(8,128)}, u32[]{:S(2)}) copy-start(f32[2,30,32,128]{3,2,1,0:T(8,128)} %param.6) | copy-start | bytes 2949124
  1.7 1.6 %copy-start.2 = (bf16[512,512]{1,0:T(8,128)(2,1)S(1)}, bf16[512,512]{1,0:T(8,128)(2,1)}, u32[]{:S(2)}) copy-start(bf16[512,512]{1,0:T(8,128)(2,1)} %w2_ref.1) | copy-start | bytes 1572868
  1.7 1.6 %copy-start.3 = (s32[32,128]{1,0:T(8,128)S(1)}, s32[32,128]{1,0:T(8,128)}, u32[]{:S(2)}) copy-start(s32[32,128]{1,0:T(8,128)} %mask_ref.1) | copy-start | bytes 49156

commit v4 on v3

--- a/solution.py
+++ b/solution.py
@@ -105,11 +105,11 @@
             pack[side, DEEP + row] = jnp.where(first_half, halves[0], halves[1])
 
     def fill(i, carry):
-        fill_row(2 * i)
-        fill_row(2 * i + 1)
-        return carry
-
-    lax.fori_loop(0, rows // 2, fill, 0)
+        for k in range(4):
+            fill_row(4 * i + k)
+        return carry
+
+    lax.fori_loop(0, rows // 4, fill, 0)
 
     peers = 3 + jnp.where(has_north, 1, 0) + jnp.where(has_south, 1, 0)
     pl.semaphore_wait(barrier, peers)
@@ -198,11 +198,11 @@
         return carry
 
     def strips_four(i, carry):
-        for k in range(4):
-            strips(DEEP + 4 * i + k, carry)
-        return carry
-
-    lax.fori_loop(0, rows // 4, strips_four, 0)
+        for k in range(8):
+            strips(DEEP + 8 * i + k, carry)
+        return carry
+
+    lax.fori_loop(0, rows // 8, strips_four, 0)
 
     @pl.when(has_south)
     def _():
@@ -247,16 +247,16 @@
         )
 
     def substep(src, dst, s):
-        first = 1 + s // 2 * 2
+        first = 1
         count = 2 * DEEP + rows + 1 - 2 * first - 1
 
         def body(i, carry):
-            row = first + 4 * i
-            for k, at, new in advance(src, w, row, [keep(row + k) for k in range(4)]):
+            row = first + 8 * i
+            for k, at, new in advance(src, w, row, [keep(row + k) for k in range(8)]):
                 dst[row + k, at : at + 8, :] = new
             return carry
 
-        lax.fori_loop(0, count // 4, body, 0)
+        lax.fori_loop(0, count // 8, body, 0)
 
     substep(x, y, 0)
     substep(y, x, 1)
@@ -352,7 +352,7 @@
             emit(me * share + row, tend[row, half])
         return carry
 
-    lax.fori_loop(0, steps, physics, 0)
+    lax.fori_loop(0, steps, physics, 0, unroll=True)
 
     def finish(g, carry):
         returned(g).wait_recv()

time: 39.8 us -> 39.1 us (0.982)
  Pallas kernels: 35.4 us -> 34.7 us
    pallas_call x1, Pallas kernels: 35.4 us -> 34.7 us  [shards(): pl.pallas_call(functools.partial(kernel, (levels, rows, lane)), out_shape...]
where the time goes in v4:
time: 39.1 us; the launch traced here: 38.9 us
  Pallas kernels  34.7 us (89%)
  local copies, waits for them, and re-layouts  4.16 us (11%)
    pallas_call x1, Pallas kernels, shards(): pl.pallas_call(functools.partial(kernel, (levels, rows, lane)), out_shape...  34.7 us
    unnamed x13, local copies, waits for them, and re-layouts  2.42 us
    reshape x1, local copies, waits for them, and re-layouts, shards(): first_weight.reshape(9, fields, lev, levels, width).transpose(0, 2, 1, 3, 4)  1.42 us

profile of v4, /device:TPU:0, one launch (start us, length us, event | category | flops | bytes accessed | tf_op | source)
XLA Modules:
  0.0 38.9 jit_solution(16627486244719611641)
XLA Ops:
  0.0 1.4 %reshape.23 = bf16[9,2,2,30,512]{4,3,2,1,0:T(8,128)(2,1)S(1)} reshape(bf16[1080,512]{1,0:T(8,128)(2,1)} %param.9) | data formatting | bytes 2211840 | tf_op jit(solution)/shard_map/reshape | solution.py:379
  1.4 0.1 copy.12
  1.5 0.0 copy-start.4
  1.5 0.0 copy-start.1
  1.5 0.1 pad.8.clone
  1.7 0.0 copy-start
  1.7 0.0 copy-start.2
  1.7 0.0 copy-start.3
  1.7 0.8 %copy-done.4 = bf16[2,512,120]{1,2,0:T(8,128)(2,1)S(1)} copy-done((bf16[2,512,120]{1,2,0:T(8,128)(2,1)S(1)}, bf16[2,512,120]{1,2,0:T(8,128)(2,1)}, u32[]{:S(2)}) %copy-start.4) | copy-done | bytes 245784
  2.5 0.2 copy.10
  2.7 0.1 copy-done.1
  2.9 0.3 copy-done
  3.2 0.1 copy-done.2
  3.3 0.0 copy-done.3
  3.3 34.7 %shard_map.64 = f32[2,960,128]{2,1,0:T(8,128)S(1)} custom-call(f32[2,960,128]{2,1,0:T(8,128)S(1)} %bitcast.13, f32[2,960,128]{2,1,0:T(8,128)S(1)} %bitcast.14, s32[32,128]{1,0:T(8,128)S(1)} %copy-done.3, bf16[1152,512]{1,0:T(8,128)(2,1)S(1)} %bitcast.10, bf16[512,512]{1,0:T(8,128)(2,1)S(1)} %copy-done.2, bf16[256,512]{1,0:T(8,128)(2,1)S(1)} %bitcast.12), custom_call_target="tpu_custom_call" | custom-call | tf_op jit(solution)/shard_map/pallas_call | solution.py:387
  38.0 0.9 %copy.15 = f32[2,30,32,128]{3,2,1,0:T(8,128)} copy(f32[2,30,32,128]{3,2,1,0:T(8,128)S(1)} %bitcast.11) | data formatting | bytes 1966080
  (2 shorter events, 0.1 us)
Async XLA Ops:
  1.5 0.9 %copy-start.4 = (bf16[2,512,120]{1,2,0:T(8,128)(2,1)S(1)}, bf16[2,512,120]{1,2,0:T(8,128)(2,1)}, u32[]{:S(2)}) copy-start(bf16[2,512,120]{1,2,0:T(8,128)(2,1)} %param.11) | copy-start | bytes 737284
  1.5 1.3 %copy-start.1 = (f32[2,30,32,128]{3,2,1,0:T(8,128)S(1)}, f32[2,30,32,128]{3,2,1,0:T(8,128)}, u32[]{:S(2)}) copy-start(f32[2,30,32,128]{3,2,1,0:T(8,128)} %param.7) | copy-start | bytes 2949124
  1.7 1.5 %copy-start = (f32[2,30,32,128]{3,2,1,0:T(8,128)S(1)}, f32[2,30,32,128]{3,2,1,0:T(8,128)}, u32[]{:S(2)}) copy-start(f32[2,30,32,128]{3,2,1,0:T(8,128)} %param.6) | copy-start | bytes 2949124
  1.7 1.6 %copy-start.2 = (bf16[512,512]{1,0:T(8,128)(2,1)S(1)}, bf16[512,512]{1,0:T(8,128)(2,1)}, u32[]{:S(2)}) copy-start(bf16[512,512]{1,0:T(8,128)(2,1)} %w2_ref.1) | copy-start | bytes 1572868
  1.7 1.6 %copy-start.3 = (s32[32,128]{1,0:T(8,128)S(1)}, s32[32,128]{1,0:T(8,128)}, u32[]{:S(2)}) copy-start(s32[32,128]{1,0:T(8,128)} %mask_ref.1) | copy-start | bytes 49156

commit v5 on v4

--- a/solution.py
+++ b/solution.py
@@ -289,21 +289,21 @@
                     jnp.bfloat16
                 )
 
-    def merge_from(start, count):
+    def merge_from(start, count, each):
         def body(i, carry):
-            merge_row(start + 2 * i)
-            merge_row(start + 2 * i + 1)
+            for k in range(each):
+                merge_row(start + each * i + k)
             return carry
 
-        lax.fori_loop(0, count // 2, body, 0)
+        lax.fori_loop(0, count // each, body, 0)
 
     mine = pl.ds(me * share, share + 2)
     theirs = pl.ds((1 - me) * share, share + 2)
     half = pl.ds(me * 2 * LP, 2 * LP)
     over = remote(cols.at[theirs], feats.at[:, :, half], 10, partner)
-    merge_from((1 - me) * share, share + 2)
+    merge_from((1 - me) * share, share + 2, 3)
     over.start()
-    merge_from(me * (share + 2), share)
+    merge_from(me * (share + 2), share, 4)
     own = pltpu.make_async_copy(cols.at[mine], feats.at[:, :, half], send.at[11])
     own.start()
     own.wait()

time: 39.1 us -> 38.7 us (0.990)
  Pallas kernels: 34.7 us -> 34.3 us
    pallas_call x1, Pallas kernels: 34.7 us -> 34.3 us  [shards(): pl.pallas_call(functools.partial(kernel, (levels, rows, lane)), out_shape...]
where the time goes in v5:
time: 38.7 us; the launch traced here: 38.5 us
  Pallas kernels  34.3 us (89%)
  local copies, waits for them, and re-layouts  4.16 us (11%)
    pallas_call x1, Pallas kernels, shards(): pl.pallas_call(functools.partial(kernel, (levels, rows, lane)), out_shape...  34.3 us
    unnamed x13, local copies, waits for them, and re-layouts  2.42 us
    reshape x1, local copies, waits for them, and re-layouts, shards(): first_weight.reshape(9, fields, lev, levels, width).transpose(0, 2, 1, 3, 4)  1.42 us

profile of v5, /device:TPU:0, one launch (start us, length us, event | category | flops | bytes accessed | tf_op | source)
XLA Modules:
  0.0 38.5 jit_solution(9940264821257466843)
XLA Ops:
  0.0 1.4 %reshape.23 = bf16[9,2,2,30,512]{4,3,2,1,0:T(8,128)(2,1)S(1)} reshape(bf16[1080,512]{1,0:T(8,128)(2,1)} %param.9) | data formatting | bytes 2211840 | tf_op jit(solution)/shard_map/reshape | solution.py:379
  1.4 0.1 copy.12
  1.5 0.0 copy-start.4
  1.5 0.0 copy-start.1
  1.5 0.1 pad.8.clone
  1.7 0.0 copy-start
  1.7 0.0 copy-start.2
  1.7 0.0 copy-start.3
  1.7 0.8 %copy-done.4 = bf16[2,512,120]{1,2,0:T(8,128)(2,1)S(1)} copy-done((bf16[2,512,120]{1,2,0:T(8,128)(2,1)S(1)}, bf16[2,512,120]{1,2,0:T(8,128)(2,1)}, u32[]{:S(2)}) %copy-start.4) | copy-done | bytes 245784
  2.5 0.2 copy.10
  2.7 0.1 copy-done.1
  2.9 0.3 copy-done
  3.2 0.1 copy-done.2
  3.3 0.0 copy-done.3
  3.3 34.3 %shard_map.64 = f32[2,960,128]{2,1,0:T(8,128)S(1)} custom-call(f32[2,960,128]{2,1,0:T(8,128)S(1)} %bitcast.13, f32[2,960,128]{2,1,0:T(8,128)S(1)} %bitcast.14, s32[32,128]{1,0:T(8,128)S(1)} %copy-done.3, bf16[1152,512]{1,0:T(8,128)(2,1)S(1)} %bitcast.10, bf16[512,512]{1,0:T(8,128)(2,1)S(1)} %copy-done.2, bf16[256,512]{1,0:T(8,128)(2,1)S(1)} %bitcast.12), custom_call_target="tpu_custom_call" | custom-call | tf_op jit(solution)/shard_map/pallas_call | solution.py:387
  37.6 0.9 %copy.15 = f32[2,30,32,128]{3,2,1,0:T(8,128)} copy(f32[2,30,32,128]{3,2,1,0:T(8,128)S(1)} %bitcast.11) | data formatting | bytes 1966080
  (2 shorter events, 0.1 us)
Async XLA Ops:
  1.5 0.9 %copy-start.4 = (bf16[2,512,120]{1,2,0:T(8,128)(2,1)S(1)}, bf16[2,512,120]{1,2,0:T(8,128)(2,1)}, u32[]{:S(2)}) copy-start(bf16[2,512,120]{1,2,0:T(8,128)(2,1)} %param.11) | copy-start | bytes 737284
  1.5 1.3 %copy-start.1 = (f32[2,30,32,128]{3,2,1,0:T(8,128)S(1)}, f32[2,30,32,128]{3,2,1,0:T(8,128)}, u32[]{:S(2)}) copy-start(f32[2,30,32,128]{3,2,1,0:T(8,128)} %param.7) | copy-start | bytes 2949124
  1.7 1.5 %copy-start = (f32[2,30,32,128]{3,2,1,0:T(8,128)S(1)}, f32[2,30,32,128]{3,2,1,0:T(8,128)}, u32[]{:S(2)}) copy-start(f32[2,30,32,128]{3,2,1,0:T(8,128)} %param.6) | copy-start | bytes 2949124
  1.7 1.6 %copy-start.2 = (bf16[512,512]{1,0:T(8,128)(2,1)S(1)}, bf16[512,512]{1,0:T(8,128)(2,1)}, u32[]{:S(2)}) copy-start(bf16[512,512]{1,0:T(8,128)(2,1)} %w2_ref.1) | copy-start | bytes 1572868
  1.7 1.6 %copy-start.3 = (s32[32,128]{1,0:T(8,128)S(1)}, s32[32,128]{1,0:T(8,128)}, u32[]{:S(2)}) copy-start(s32[32,128]{1,0:T(8,128)} %mask_ref.1) | copy-start | bytes 49156
